TPU v7x, 256 devices: a whole 4x4x8 slice. The times are simulated.
256 devices in a mesh: space: 128 (over x_lo, z, y, core), dp: 2 (over x_hi).
Axes of the slice: x: 4 (x_hi: 2, x_lo: 2; x = x_hi * 2 + x_lo), y: 4, z: 8, core: 2. Of those that a mesh axis runs over, the one named last changes fastest.
Arguments:
- cell_state: bfloat16 [2, 256, 32, 32, 128], P('dp', 'space'), may hold values from -6 to 6
- cotangent: bfloat16 [2, 256, 32, 32, 128], P('dp', 'space'), may hold values from -6 to 6
- kernels: bfloat16 [2, 3, 3, 128, 128], replicated, may hold values from -0.1875 to 0.1875
- slot_of_tile: int32 [192], replicated, may hold values from 0 to 255, as said below
- neighbours: int32 [192, 8], replicated, may hold values from 0 to 191, as said below
- rotations: int32 [192, 8], replicated, may hold values from 0 to 3
- corner_flags: int32 [192, 4], replicated, may hold values 0 or 1
Outputs:
- next_state: bfloat16 [2, 256, 32, 32, 128], P('dp', 'space')
- cell_grad: bfloat16 [2, 256, 32, 32, 128], P('dp', 'space')
- kernel_grads: float32 [2, 3, 3, 128, 128], replicated
Inputs may be any that keep to these rules, and one draw needn't show every extreme that they name: `slot_of_tile`: distinct tiles take distinct slots; slot s lies on space index s // 2; space indices 2p and 2p + 1 together hold three tiles: one of the two indices holds two of them, the other one. neighbours[t, k] for k < 4 is the tile across edge k of tile t, for k >= 4 the tile across corner k - 4, in the tile's own frame; each lies on a space index at most 3 away from tile t's, counted cyclically, and that distance occurs in every draw.
All inputs are finite; a program needn't handle non-finite values.
Results may differ from a plain program's by a relative error of at most 0.011.
Values may be sent and summed in bfloat16 or wider, within the bound.
A program may use at most 128 MiB of HBM per device.

v0:
```python
import functools
import math

import jax
import jax.numpy as jnp
import numpy as np
from jax import lax
from jax.experimental import pallas as pl
from jax.experimental.pallas import tpu as pltpu
from jax.sharding import PartitionSpec as P

RES_BLOCKS = 1
DILATION_ONE = 2
DILATION_TWO = 4
REACH_DEV = 3


CONV_AXES = ("NHWC", "HWIO", "NHWC")


def as_sent(shard):

    def short(part):
        return part.astype(jnp.bfloat16) if part.dtype == jnp.float32 else part

    return jax.tree.map(short, shard)


def shifted(value, axis, steps):
    count = lax.axis_size(axis)
    pairs = [(source, (source + steps) % count) for source in range(count)]
    return lax.ppermute(value, axis, pairs)


def boundary(tile_data, rim_depth):
    extent = tile_data.shape[3]
    far = extent - rim_depth
    sides = [
        tile_data[:, :, :rim_depth],
        tile_data[:, :, :, far:],
        tile_data[:, :, far:],
        tile_data[:, :, :, :rim_depth],
    ]
    blocks = [
        tile_data[:, :, :rim_depth, far:],
        tile_data[:, :, far:, far:],
        tile_data[:, :, far:, :rim_depth],
        tile_data[:, :, :rim_depth, :rim_depth],
    ]
    strips = jnp.stack(
        [jnp.rot90(sides[quarter], quarter, axes=(2, 3)) for quarter in range(4)], axis=2
    )
    corners = jnp.stack(
        [jnp.rot90(blocks[quarter], quarter, axes=(2, 3))[:, :, :, ::-1] for quarter in range(4)],
        axis=2,
    )
    return (strips, corners)


def assemble(tile_data, strips, corners):
    edge_parts = [
        jnp.rot90(strips[:, :, quarter, ::-1, ::-1], -quarter, axes=(2, 3)) for quarter in range(4)
    ]
    corner_parts = [
        jnp.rot90(corners[:, :, quarter, ::-1], -quarter, axes=(2, 3)) for quarter in range(4)
    ]
    top_row = jnp.concatenate([corner_parts[3], edge_parts[0], corner_parts[0]], axis=3)
    middle = jnp.concatenate([edge_parts[3], tile_data, edge_parts[1]], axis=3)
    bottom = jnp.concatenate([corner_parts[2], edge_parts[2], corner_parts[1]], axis=3)
    return jnp.concatenate([top_row, middle, bottom], axis=2)


def rim_pieces(tile_data, rim_depth):
    strips, corners = boundary(tile_data, rim_depth)
    joined = jnp.concatenate([strips, corners], axis=4)
    return joined.reshape((joined.shape[0], joined.shape[1] * 4) + joined.shape[3:])


def conv_apply(padded, kernel, spread):
    merged = padded.reshape((-1,) + padded.shape[2:])
    result = lax.conv_general_dilated(
        merged,
        kernel,
        (1, 1),
        "VALID",
        rhs_dilation=(spread, spread),
        dimension_numbers=CONV_AXES,
        preferred_element_type=jnp.float32,
    )
    return result.reshape(padded.shape[:2] + result.shape[1:])


def conv_back(grad_out, kernel, spread):
    merged = grad_out.reshape((-1,) + grad_out.shape[2:])
    flipped = jnp.swapaxes(kernel[::-1, ::-1], 2, 3)
    margin = 2 * spread
    result = lax.conv_general_dilated(
        merged,
        flipped,
        (1, 1),
        ((margin, margin), (margin, margin)),
        rhs_dilation=(spread, spread),
        dimension_numbers=CONV_AXES,
        preferred_element_type=jnp.float32,
    )
    return result.reshape(grad_out.shape[:2] + result.shape[1:])


def kernel_grad(padded, grad_out, spread):
    extent = grad_out.shape[2]
    tap_terms = []
    for row_tap in range(3):
        for col_tap in range(3):
            window = padded[
                :,
                :,
                row_tap * spread : row_tap * spread + extent,
                col_tap * spread : col_tap * spread + extent,
            ]
            tap_terms.append(
                lax.dot_general(
                    window,
                    grad_out,
                    (((0, 1, 2, 3), (0, 1, 2, 3)), ((), ())),
                    preferred_element_type=jnp.float32,
                )
            )
    stacked = jnp.stack(tap_terms)
    return stacked.reshape((3, 3) + stacked.shape[1:])


def halo_plan(slot_of_tile, neighbours, rotations, corner_flags, slot_count):
    span_count = lax.axis_size("space")
    myself = lax.axis_index("space")
    tile_count = slot_of_tile.shape[0]
    owned = myself * slot_count + jnp.arange(slot_count, dtype=jnp.int32)
    matches = slot_of_tile[None, :] == owned[:, None]
    present = jnp.any(matches, axis=1)
    tile_here = jnp.sum(
        jnp.where(matches, jnp.arange(tile_count, dtype=jnp.int32)[None, :], 0), axis=1
    )
    nearby = jnp.take(neighbours, tile_here, axis=0)
    turn_code = jnp.take(rotations, tile_here, axis=0)
    facing = (jnp.arange(8, dtype=jnp.int32)[None, :] % 4 + 2 + turn_code) % 4
    source = jnp.take(slot_of_tile, nearby)
    holder = source // slot_count
    within = source % slot_count
    offset = jnp.clip(
        (myself - holder + span_count + REACH_DEV) % span_count - REACH_DEV, -REACH_DEV, REACH_DEV
    )
    select = ((offset + REACH_DEV) * slot_count + within) * 4 + facing
    keep_corner = jnp.take(corner_flags, tile_here, axis=0) == 0
    return (select[:, :4].reshape(-1), select[:, 4:].reshape(-1), keep_corner.reshape(-1), present)


def fetch_near(bundle):
    arrived = {0: bundle}
    for offset in list(range(-REACH_DEV, 0)) + list(range(1, REACH_DEV + 1)):
        arrived[offset] = shifted(as_sent(bundle), "space", offset).astype(bundle.dtype)
    return [arrived[offset] for offset in range(-REACH_DEV, REACH_DEV + 1)]


def return_near(parts):
    total = parts[0]
    for offset in list(range(-REACH_DEV, 0)) + list(range(1, REACH_DEV + 1)):
        total = total + shifted(parts[offset].astype(jnp.bfloat16), "space", -offset).astype(
            jnp.float32
        )
    return total


def halo_forward(tile_data, rim_depth, plan):
    pick_edge, pick_corner, keep_corner = plan[:3]
    samples_here, slot_count, extent = (tile_data.shape[0], tile_data.shape[1], tile_data.shape[2])
    channels = tile_data.shape[4]
    gathered = jnp.concatenate(fetch_near(rim_pieces(tile_data, rim_depth)), axis=1)
    edge_part = jnp.take(gathered, pick_edge, axis=1)[:, :, :, :extent]
    corner_part = jnp.take(gathered, pick_corner, axis=1)[:, :, :, extent:]
    corner_part = jnp.where(
        keep_corner[None, :, None, None, None], corner_part, jnp.zeros((), corner_part.dtype)
    )
    strips = edge_part.reshape(samples_here, slot_count, 4, rim_depth, extent, channels)
    corners = corner_part.reshape(samples_here, slot_count, 4, rim_depth, rim_depth, channels)
    return assemble(tile_data, strips, corners)


def halo_backward(grad_wide, rim_depth, plan):
    pick_edge, pick_corner, keep_corner = plan[:3]
    samples_here, slot_count = (grad_wide.shape[0], grad_wide.shape[1])
    extent = grad_wide.shape[2] - 2 * rim_depth
    channels = grad_wide.shape[4]
    tile_zero = jnp.zeros((samples_here, slot_count, extent, extent, channels), jnp.float32)
    strip_zero = jnp.zeros((samples_here, slot_count, 4, rim_depth, extent, channels), jnp.float32)
    corner_zero = jnp.zeros(
        (samples_here, slot_count, 4, rim_depth, rim_depth, channels), jnp.float32
    )
    _, assemble_back = jax.vjp(assemble, tile_zero, strip_zero, corner_zero)
    grad_tiles, grad_strips, grad_corners = assemble_back(grad_wide)
    pieces = slot_count * 4
    grad_corners = grad_corners.reshape(samples_here, pieces, rim_depth, rim_depth, channels)
    grad_corners = jnp.where(keep_corner[None, :, None, None, None], grad_corners, 0.0)
    spread_out = jnp.zeros(
        (samples_here, (2 * REACH_DEV + 1) * pieces, rim_depth, extent + rim_depth, channels),
        jnp.float32,
    )
    spread_out = spread_out.at[:, pick_edge, :, :extent].add(
        grad_strips.reshape(samples_here, pieces, rim_depth, extent, channels)
    )
    spread_out = spread_out.at[:, pick_corner, :, extent:].add(grad_corners)
    parts = {
        offset: spread_out[:, (offset + REACH_DEV) * pieces : (offset + REACH_DEV + 1) * pieces]
        for offset in range(-REACH_DEV, REACH_DEV + 1)
    }
    returned = return_near(parts)
    _, rim_back = jax.vjp(lambda tile_part: rim_pieces(tile_part, rim_depth), tile_zero)
    return grad_tiles + rim_back(returned)[0]


def shards(cell_state, cotangent, kernels, slot_of_tile, neighbours, rotations, corner_flags):
    plan = halo_plan(slot_of_tile, neighbours, rotations, corner_flags, cell_state.shape[1])
    keep_slot = plan[3][None, :, None, None, None]
    current = cell_state
    block_at = 0
    widened = halo_forward(current, DILATION_ONE, plan)
    before = conv_apply(widened, kernels[2 * block_at], DILATION_ONE)
    hidden = jax.nn.gelu(before).astype(jnp.bfloat16)
    widened_two = halo_forward(hidden, DILATION_TWO, plan)
    branch = conv_apply(widened_two, kernels[2 * block_at + 1], DILATION_TWO)
    stored = [(widened, before, widened_two)]
    current = (current.astype(jnp.float32) + branch).astype(jnp.bfloat16)
    next_state = jnp.where(keep_slot, current, jnp.zeros((), jnp.bfloat16))
    gradient = jnp.where(keep_slot, cotangent, jnp.zeros((), jnp.bfloat16))
    kernel_terms = [None] * (2 * RES_BLOCKS)
    extent = cell_state.shape[2]
    norm_scale = 1.0 / math.sqrt(
        cell_state.shape[0] * lax.axis_size("dp") * slot_of_tile.shape[0] * extent * extent
    )
    for block_at in reversed(range(RES_BLOCKS)):
        widened, before, widened_two = stored[block_at]
        outer_term = kernel_grad(widened_two, gradient, DILATION_TWO)
        kernel_terms[2 * block_at + 1] = outer_term
        grad_hidden = halo_backward(
            conv_back(gradient, kernels[2 * block_at + 1], DILATION_TWO), DILATION_TWO, plan
        ).astype(jnp.bfloat16)
        _, gelu_back = jax.vjp(jax.nn.gelu, before)
        grad_before = gelu_back(grad_hidden.astype(jnp.float32))[0].astype(jnp.bfloat16)
        inner_term = kernel_grad(widened, grad_before, DILATION_ONE)
        kernel_terms[2 * block_at] = inner_term
        returned = halo_backward(
            conv_back(grad_before, kernels[2 * block_at], DILATION_ONE), DILATION_ONE, plan
        )
        gradient = (gradient.astype(jnp.float32) + returned).astype(jnp.bfloat16)
    stacked = jnp.stack(kernel_terms)
    stacked = lax.psum(stacked, ("space", "dp"))
    return (next_state, gradient, stacked * norm_scale)


MESH_ID = pl.DeviceIdType.MESH
SPAN = 128
STRIP_CAP = (1, 2, 2, 2, 2, 1)
CORNER_CAP = 4
PART = 20
OFFSETS = (-3, -2, -1, 1, 2, 3)
ORDER = (2, 3, 1, 4, 0, 5)
SELF = 6
NOT_STRIP, NOT_CORNER = 20, 32
T_STRIP_LIST, T_CORNER_LIST, T_GIVE_STRIP, T_GIVE_CORNER = 0, 12, 36, 48
T_ADD_STRIP, T_ADD_CORNER, T_PIECES, T_PRESENT = 72, 88, 104, 200
T_OVER, T_SPARE, T_COUNT, T_SIZE = 202, 203, 208, 224
VMEM_BYTES = 56 * 1024 * 1024
F32 = jnp.float32
BF16 = jnp.bfloat16


def cell_order():
    rows, cols = np.meshgrid(np.arange(4), np.arange(4), indexing="ij")
    return ((cols // 2) * 8 + (rows // 2) * 4 + (rows % 2) * 2 + cols % 2).astype(np.int64)


def permutations():
    order = cell_order()
    to_blocks = np.zeros((128, 128), np.float32)
    for row in range(4):
        for col in range(32):
            to_blocks[(col // 4) * 16 + order[row, col % 4], row * 32 + col] = 1
    mats = [to_blocks, to_blocks.T]
    for turn in range(4):
        turned = np.rot90(order, turn)
        small = np.zeros((16, 16), np.float32)
        small[order.reshape(-1), turned.reshape(-1)] = 1
        for flip in range(2):
            line = np.eye(8)[::-1] if flip else np.eye(8)
            mats.append(np.kron(line, small))
    return np.stack(mats)


def turn_matrix(turn, flip):
    return 2 + 2 * turn + flip


def flips(edge, turn):
    side = (edge + 2 + turn) & 1
    once = jnp.where((turn == 1) & (side == 0), 1, 0)
    thrice = jnp.where((turn == 3) & (side == 1), 1, 0)
    return jnp.where(turn == 2, 1, once + thrice)


def plan_kernel(slot_ref, near_ref, turn_ref, flag_ref, table, tile_at):
    me = lax.axis_index("space")
    for entry in range(T_SIZE):
        table[entry] = 0
    for entry in range(16):
        table[T_ADD_STRIP + entry] = NOT_STRIP
        table[T_ADD_CORNER + entry] = NOT_CORNER
    for rel in range(14):
        tile_at[(me + rel // 2 - 3 + SPAN) % SPAN * 2 + rel % 2] = -1

    def place(step, carry):
        for inner in range(16):
            tile = step * 16 + inner
            tile_at[slot_ref[tile]] = tile
        return carry

    lax.fori_loop(0, slot_ref.shape[0] // 16, place, 0)
    over = jnp.int32(0)

    def contribute(hit, kind, entry, code):
        counter = T_COUNT + kind * 8 + entry
        count = table[counter]
        table[jnp.where(hit, counter, T_SPARE)] = count + 1
        place_at = (T_ADD_CORNER if kind else T_ADD_STRIP) + entry * 2 + jnp.minimum(count, 1)
        table[jnp.where(hit, place_at, T_SPARE)] = code
        return jnp.where(hit & (count > 1), 1, 0)

    for where, offset in enumerate(OFFSETS):
        seen = [jnp.int32(0), jnp.int32(0)]
        for slot in range(2):
            tile = tile_at[(me + offset + SPAN) % SPAN * 2 + slot]
            row = jnp.maximum(tile, 0)
            for piece in range(8):
                kind = piece // 4
                source = slot_ref[near_ref[row, piece]]
                hit = (tile >= 0) & (source // 2 == me)
                entry = source % 2 * 4 + ((piece + 2 + turn_ref[row, piece]) & 3)
                cap = CORNER_CAP if kind else STRIP_CAP[where]
                rank = jnp.minimum(seen[kind], cap - 1)
                over = over + jnp.where(hit & (seen[kind] >= cap), 1, 0)
                seen[kind] = seen[kind] + jnp.where(hit, 1, 0)
                width = 4 if kind else 2
                place_at = (T_CORNER_LIST if kind else T_STRIP_LIST) + where * width + rank
                table[jnp.where(hit, place_at, T_SPARE)] = entry
                over = over + contribute(hit, kind, entry, where * width + rank)
    seen = [[jnp.int32(0)] * 7, [jnp.int32(0)] * 7]
    for slot in range(2):
        tile = tile_at[me * 2 + slot]
        row = jnp.maximum(tile, 0)
        valid = jnp.where(tile >= 0, 1, 0)
        table[T_PRESENT + slot] = valid
        for piece in range(8):
            kind = piece // 4
            source = slot_ref[near_ref[row, piece]]
            turn = turn_ref[row, piece] & 3
            offset = jnp.clip((source // 2 - me + 3 + SPAN) % SPAN, 0, 6)
            where = jnp.where(offset == 3, SELF, jnp.where(offset < 3, offset, offset - 1))
            rank = jnp.int32(0)
            for choice in range(7):
                match = jnp.where(offset == choice, valid, 0)
                rank = rank + match * seen[kind][choice]
                seen[kind][choice] = seen[kind][choice] + match
            rank = jnp.minimum(rank, 3 if kind else 1)
            keep = valid
            if kind:
                keep = valid * jnp.where(flag_ref[row, piece - 4] == 0, 1, 0)
            entry = source % 2 * 4 + ((piece + 2 + turn) & 3)
            base = T_PIECES + (slot * 8 + piece) * 6
            table[base] = valid
            table[base + 1] = where
            table[base + 2] = rank
            table[base + 3] = turn
            table[base + 4] = entry
            table[base + 5] = keep
            mine = slot * 4 + piece % 4
            own = (valid > 0) & (where == SELF)
            away = (valid > 0) & (where != SELF)
            place_at = (T_GIVE_CORNER if kind else T_GIVE_STRIP) + where * (4 if kind else 2) + rank
            table[jnp.where(away, place_at, T_SPARE)] = mine
            over = over + contribute(own, kind, entry, (24 if kind else 12) + mine)
    table[T_OVER] = over


def piece_of(table, slot, piece):
    base = T_PIECES + (slot * 8 + piece) * 6
    return [table[base + field] for field in range(6)]


def blocks(value):
    return value.reshape((-1, 16, 128))


def cells(value):
    return value.reshape((-1, 128))


def product(left, right):
    return jnp.dot(left, right, preferred_element_type=F32)


EDGE_OF = ((0, slice(None)), (slice(None), 7), (7, slice(None)), (slice(None), 0))
CORNER_OF = ((0, 7), (7, 7), (7, 0), (0, 0))
BAND_OF = ((0, slice(1, 9)), (slice(1, 9), 9), (9, slice(1, 9)), (slice(1, 9), 0))
BLOCK_OF = ((0, 9), (9, 9), (9, 0), (0, 0))


def take_rims(tile_ref, strips, corners):
    for slot in range(2):
        for side in range(4):
            strips[slot * 4 + side] = blocks(tile_ref[(slot,) + EDGE_OF[side]])
            corners[slot * 4 + side] = tile_ref[(slot,) + CORNER_OF[side]]


def send_rims(table, strips, corners, send, strip_list=T_STRIP_LIST, corner_list=T_CORNER_LIST):
    for where in range(6):
        for rank in range(STRIP_CAP[where]):
            send[where, 4 + rank * 8 : 12 + rank * 8] = strips[table[strip_list + where * 2 + rank]]
        for rank in range(CORNER_CAP):
            send[where, rank] = corners[table[corner_list + where * 4 + rank]]


def corner_turns(table, turns, back):
    parts = []
    for slot in range(2):
        for side in range(4):
            fields = piece_of(table, slot, 4 + side)
            turn = (4 - fields[3]) & 3 if back else fields[3]
            rows = turns[turn_matrix(turn, 0)]
            at = (slot * 4 + side) * 16
            parts.append(rows[at : at + 16] * jnp.where(fields[5] > 0, 1.0, 0.0).astype(BF16))
    return jnp.concatenate(parts, axis=0)


def widen(table, tile_ref, strips, corners, arrived, turns, padded):
    for slot in range(2):
        padded[slot, 1:9, 1:9] = tile_ref[slot]
        for edge in range(4):
            valid, where, rank, turn, entry, keep = piece_of(table, slot, edge)
            own = strips[entry]
            other = arrived[jnp.minimum(where, 5), pl.ds(4 + rank * 8, 8)]
            strip = jnp.where(where == SELF, own, other)
            strip = jnp.where(valid > 0, strip, jnp.zeros_like(strip))
            turned = product(turns[turn_matrix(turn, flips(edge, turn))], cells(strip))
            padded[(slot,) + BAND_OF[edge]] = blocks(turned.astype(BF16))
    stack = []
    for slot in range(2):
        for side in range(4):
            valid, where, rank, turn, entry, keep = piece_of(table, slot, 4 + side)
            block = jnp.where(where == SELF, corners[entry], arrived[jnp.minimum(where, 5), rank])
            stack.append(jnp.where(valid > 0, block, jnp.zeros_like(block)))
    turned = product(corner_turns(table, turns, False), jnp.concatenate(stack, axis=0))
    turned = blocks(turned.astype(BF16))
    for slot in range(2):
        for side in range(4):
            padded[(slot,) + BLOCK_OF[side]] = turned[slot * 4 + side]


def give_back(table, wide, turns, send, strips, corners):
    for slot in range(2):
        for edge in range(4):
            valid, where, rank, turn, entry, keep = piece_of(table, slot, edge)
            band = cells(blocks(wide[(slot,) + BAND_OF[edge]])).astype(BF16)
            turned = product(turns[turn_matrix((4 - turn) & 3, flips(edge, turn))], band)
            strips[slot * 4 + edge] = blocks(turned.astype(BF16))
    stack = [wide[(slot,) + BLOCK_OF[side]].astype(BF16) for slot in range(2) for side in range(4)]
    turned = product(corner_turns(table, turns, True), jnp.concatenate(stack, axis=0))
    corners[...] = blocks(turned.astype(BF16))
    send_rims(table, strips, corners, send, T_GIVE_STRIP, T_GIVE_CORNER)


def take_back(table, arrived, strips, corners, total):
    for slot in range(2):
        for side in range(4):
            at = (slot,) + EDGE_OF[side]
            value = total[at]
            for extra in range(2):
                code = table[T_ADD_STRIP + (slot * 4 + side) * 2 + extra]
                far = jnp.minimum(code, 11)
                near = jnp.clip(code - 12, 0, 7)
                part = jnp.where(code < 12, arrived[far // 2, pl.ds(4 + far % 2 * 8, 8)], strips[near])
                part = jnp.where(code == NOT_STRIP, jnp.zeros_like(part), part)
                value = value + part.astype(F32)
            total[at] = value
    for slot in range(2):
        for side in range(4):
            at = (slot,) + CORNER_OF[side]
            value = total[at]
            for extra in range(2):
                code = table[T_ADD_CORNER + (slot * 4 + side) * 2 + extra]
                far = jnp.minimum(code, 23)
                near = jnp.clip(code - 24, 0, 7)
                part = jnp.where(code < 24, arrived[far // 4, far % 4], corners[near])
                part = jnp.where(code == NOT_CORNER, jnp.zeros_like(part), part)
                value = value + part.astype(F32)
            total[at] = value


def halves(value):
    return value.astype(F32).reshape(value.shape[0], value.shape[1] * 2, 8, 128)


def shifted_up(upper, lower):
    low = lax.broadcasted_iota(jnp.int32, upper.shape, upper.ndim - 2) < 4
    mixed = jnp.where(low, lower, upper)
    return jnp.concatenate([mixed[..., 4:, :], mixed[..., :4, :]], axis=mixed.ndim - 2)


def gelu_parts(value):
    root = math.sqrt(2.0 / math.pi)
    square = value * value
    bent = jnp.tanh(root * (value + 0.044715 * (value * square)))
    half = 0.5 * (1.0 + bent)
    slope = half + 0.5 * value * (1.0 - bent * bent) * (root * (1.0 + 3 * 0.044715 * square))
    return (value * half, slope)


UNITS = 72
HALF = 37
CHUNK = 3


def chunk_start(index):
    return (index * (HALF - CHUNK)) // 15


class Swap:
    def __init__(self, me, send, arrived, sems):
        self.copies = []
        for where in ORDER:
            size = 4 + 8 * STRIP_CAP[where]
            self.copies.append(
                pltpu.make_async_remote_copy(
                    src_ref=send.at[where, pl.ds(0, size)],
                    dst_ref=arrived.at[5 - where, pl.ds(0, size)],
                    send_sem=sems.at[0, where],
                    recv_sem=sems.at[1, 5 - where],
                    device_id={"space": lax.rem(me + OFFSETS[where] + SPAN, SPAN)},
                    device_id_type=MESH_ID,
                )
            )

    def start(self):
        for copy in self.copies:
            copy.start()

    def wait(self):
        for copy in self.copies:
            copy.wait()


class Place:
    def __init__(self):
        me = lax.axis_index("space")
        self.me = me
        self.core, self.y, self.z, self.x_lo = me % 2, me // 2 % 4, me // 8 % 8, me // 64
        self.plane = (lax.axis_index("dp") * 2 + self.x_lo) * 4 + self.y
        self.mate = {"space": me + 1 - 2 * self.core}

    def at_plane(self, index):
        return {
            "dp": index // 8,
            "space": ((index // 4 % 2) * 8 + self.z) * 8 + index % 4 * 2 + self.core,
        }

    def at_line(self, index):
        return {"space": (self.x_lo * 8 + index) * 8 + self.y * 2 + self.core}


class Sum:
    def __init__(self, place, buffers, sems):
        self.place = place
        self.half_send, self.half_in, self.plane_send, self.plane_in, self.line_in = buffers[:5]
        self.wide_in, self.pair_send, self.pair_in, self.acc = buffers[5:]
        self.sems = sems
        self.copies = []

    def copy(self, source, target, index, where):
        one = pltpu.make_async_remote_copy(
            src_ref=source,
            dst_ref=target,
            send_sem=self.sems.at[0, index],
            recv_sem=self.sems.at[1, index],
            device_id=where,
            device_id_type=MESH_ID,
        )
        one.start()
        self.copies.append(one)

    def put(self, index, value):
        half, at = index // 36, index % 36
        size = value.shape[0]
        self.half_send[half, at : at + size] = value.astype(BF16)

    def wait(self):
        for one in self.copies:
            one.wait()
        self.copies = []

    def one(self):
        place = self.place
        self.copy(self.half_send.at[1 - place.core], self.half_in, 0, place.mate)

    def two(self):
        place = self.place
        self.wait()
        self.acc[...] = self.half_send[place.core].astype(F32) + self.half_in[...].astype(F32)
        self.plane_send[...] = self.acc[...].astype(BF16)
        for step in range(1, 16):
            peer = lax.rem(place.plane + step, 16)
            source = self.plane_send.at[pl.ds(chunk_start(peer), CHUNK)]
            self.copy(source, self.plane_in.at[step - 1], step, place.at_plane(peer))

    def three(self):
        place = self.place
        self.wait()
        total = self.acc[pl.ds(chunk_start(place.plane), CHUNK)]
        for step in range(15):
            total = total + self.plane_in[step].astype(F32)
        self.line_in[place.z] = total.astype(BF16)
        for step in range(1, 8):
            peer = lax.rem(place.z + step, 8)
            self.copy(self.line_in.at[place.z], self.line_in.at[place.z], 15 + step, place.at_line(peer))

    def four(self):
        place = self.place
        self.wait()
        total = self.line_in[0].astype(F32)
        for index in range(1, 8):
            total = total + self.line_in[index].astype(F32)
        self.wide_in[place.plane] = total.astype(BF16)
        for step in range(1, 16):
            peer = lax.rem(place.plane + step, 16)
            here = self.wide_in.at[place.plane]
            self.copy(here, here, 22 + step, place.at_plane(peer))

    def five(self):
        self.wait()
        for index in range(16):
            at = chunk_start(index)
            self.pair_send[at : at + CHUNK] = self.wide_in[index]
        self.copy(self.pair_send, self.pair_in, 38, self.place.mate)

    def end(self, out, layer, scale, over):
        self.wait()
        core = self.place.core
        mine, other = self.pair_send[...].astype(F32), self.pair_in[...].astype(F32)
        out[layer, :36] = jnp.where(core == 0, mine[:36], other[:36]) * scale
        out[layer, 36:] = jnp.where(core == 0, other[:36], mine[:36]) * scale
        if over is not None:
            over[...] = mine[36]


def whole(
    scale, table, state, cotangent, kernels, turns, next_state, cell_grad, sums, over,
    state_blocks, grad_blocks, hidden_blocks, strips, corners, given_strips, given_corners,
    send_a, send_b, send_c, send_d, in_a, in_b, in_c, in_d,
    forward, flipped, grad_wide, wide, total, padded, even, odd, before, grad_even, grad_odd, grad_turned,
    *rest,
):
    sum_one, sum_two = rest[:9], rest[9:18]
    swap_sems, one_sems, two_sems = rest[18:]
    place = Place()
    me = place.me
    barrier = pltpu.get_barrier_semaphore()

    def greet(where):
        pl.semaphore_signal(barrier, inc=1, device_id=where, device_id_type=MESH_ID)

    for offset in OFFSETS:
        greet({"space": lax.rem(me + offset + SPAN, SPAN)})
    greet(place.mate)
    for step in range(1, 16):
        greet(place.at_plane(lax.rem(place.plane + step, 16)))
    for step in range(1, 8):
        greet(place.at_line(lax.rem(place.z + step, 8)))

    rims_one = Swap(me, send_a, in_a, swap_sems.at[0])
    back_two = Swap(me, send_b, in_b, swap_sems.at[1])
    rims_two = Swap(me, send_c, in_c, swap_sems.at[2])
    back_one = Swap(me, send_d, in_d, swap_sems.at[3])
    reduce_one = Sum(place, sum_one, one_sems)
    reduce_two = Sum(place, sum_two, two_sems)

    for slot in range(2):
        for row in range(8):
            moved = product(turns[0], state[slot, row])
            state_blocks[slot, row] = blocks(moved.astype(BF16))
    take_rims(state_blocks, strips, corners)
    send_rims(table, strips, corners, send_a)
    pl.semaphore_wait(barrier, 29)
    rims_one.start()

    for layer in range(2):
        for tap in range(9):
            weight = kernels[layer, tap // 3, tap % 3]
            forward[layer, tap * 128 : tap * 128 + 128] = weight
            flipped[layer, tap * 128 : tap * 128 + 128] = weight.astype(F32).T.astype(BF16)
    grad_wide[...] = jnp.zeros_like(grad_wide)
    for slot in range(2):
        present = jnp.where(table[T_PRESENT + slot] > 0, 1.0, 0.0)
        for row in range(8):
            moved = blocks((product(turns[0], cotangent[slot, row]) * present).astype(BF16))
            grad_blocks[slot, row] = moved
            grad_wide[slot, 2 + row, 2:10] = moved
    for slot in range(2):

        def rows_back(step, carry):
            taps = [
                cells(grad_wide[slot, pl.ds(step * 2 + 2 - up, 2), 2 - across : 12 - across])
                for up in range(3)
                for across in range(3)
            ]
            result = product(jnp.concatenate(taps, axis=1), flipped[1])
            wide[slot, pl.ds(step * 2, 2)] = result.reshape(2, 10, 16, 128)
            return carry

        lax.fori_loop(0, 5, rows_back, 0)
        total[slot] = wide[slot, 1:9, 1:9]
    give_back(table, wide, turns, send_b, given_strips, given_corners)
    back_two.start()

    rims_one.wait()
    widen(table, state_blocks, strips, corners, in_a, turns, padded)
    for row in range(10):
        both = [halves(padded[slot, row : row + 1])[0] for slot in range(2)]
        even[row] = jnp.concatenate(both, axis=1).astype(BF16)
    for row in range(9):
        both = [
            shifted_up(halves(padded[slot, row : row + 1])[0], halves(padded[slot, row + 1 : row + 2])[0])
            for slot in range(2)
        ]
        odd[row] = jnp.concatenate(both, axis=1).astype(BF16)

    def window(row, up, across, count):
        source, at = ((odd, row), (even, row + 1), (odd, row + 1))[up]
        return cells(source[pl.ds(at, count), 1 + across : 17 + across])

    def first(row, carry):
        taps = [window(row, up, across, 1) for up in range(3) for across in range(3)]
        result = product(jnp.concatenate(taps, axis=1), forward[0]).reshape(16, 16, 128)
        before[row] = result
        hidden = gelu_parts(result)[0]
        for slot in range(2):
            part = hidden[:, slot * 8 : slot * 8 + 8].reshape(8, 16, 128)
            hidden_blocks[slot, row] = part.astype(BF16)
        return carry

    lax.fori_loop(0, 8, first, 0)
    take_rims(hidden_blocks, strips, corners)
    send_rims(table, strips, corners, send_c)
    rims_two.start()

    back_two.wait()
    take_back(table, in_b, given_strips, given_corners, total)
    grad_even[...] = jnp.zeros_like(grad_even)
    grad_odd[...] = jnp.zeros_like(grad_odd)

    def pointwise(row, carry):
        both = [total[slot, row].astype(BF16).astype(F32).reshape(16, 8, 128) for slot in range(2)]
        grad = jnp.concatenate(both, axis=1) * gelu_parts(before[row])[1]
        grad = grad.astype(BF16)
        grad_even[row + 1, 2:18] = grad
        at = pl.multiple_of(row * 256, 256)
        grad_turned[:, pl.ds(at, 256)] = cells(grad).astype(F32).T.astype(BF16)
        return carry

    lax.fori_loop(0, 8, pointwise, 0)
    for row in range(9):
        low = grad_even[row, 2:18].astype(F32)
        high = grad_even[row + 1, 2:18].astype(F32)
        both = [
            shifted_up(low[:, slot * 8 : slot * 8 + 8], high[:, slot * 8 : slot * 8 + 8])
            for slot in range(2)
        ]
        grad_odd[row + 1, 2:18] = jnp.concatenate(both, axis=1).astype(BF16)

    def returned(row, carry):
        taps = []
        for up in range(3):
            source, at = ((grad_odd, row + 1), (grad_even, row), (grad_odd, row))[up]
            for across in range(3):
                taps.append(cells(source[at, 2 - across : 20 - across]))
        result = product(jnp.concatenate(taps, axis=1), flipped[0]).reshape(18, 16, 128)
        blank = jnp.zeros((1, 8, 128), F32)
        for slot in range(2):
            part = jnp.concatenate([blank, result[:, slot * 8 : slot * 8 + 8], blank], axis=0)
            wide[slot, row] = part.reshape(10, 16, 128)
        return carry

    lax.fori_loop(0, 10, returned, 0)
    give_back(table, wide, turns, send_d, given_strips, given_corners)
    back_one.start()
    for slot in range(2):
        total[slot] = wide[slot, 1:9, 1:9]

    for up in range(3):
        for across in range(3):
            term = product(grad_turned[...], window(0, up, across, 8))
            reduce_one.put((up * 3 + across) * 8, term.T.reshape(8, 16, 128)[:4])
            reduce_one.put((up * 3 + across) * 8 + 4, term.T.reshape(8, 16, 128)[4:])
    blank = jnp.zeros((1, 16, 128), F32)
    broken = blank + table[T_OVER].astype(F32)
    for half in range(2):
        reduce_one.half_send[half, 36:37] = blank.astype(BF16)
        reduce_two.half_send[half, 36:37] = broken.astype(BF16)
    reduce_one.one()

    rims_two.wait()
    widen(table, hidden_blocks, strips, corners, in_c, turns, padded)
    for slot in range(2):
        for step in range(4):
            grad = cells(grad_blocks[slot, step * 2 : step * 2 + 2])
            at = slot * 1024 + step * 256
            grad_turned[:, at : at + 256] = grad.astype(F32).T.astype(BF16)
    reduce_one.two()
    for up in range(3):
        for across in range(3):
            term = sum(
                product(
                    grad_turned[:, slot * 1024 : slot * 1024 + 1024],
                    cells(padded[slot, up : up + 8, across : across + 8]),
                )
                for slot in range(2)
            )
            reduce_two.put((up * 3 + across) * 8, term.T.reshape(8, 16, 128)[:4])
            reduce_two.put((up * 3 + across) * 8 + 4, term.T.reshape(8, 16, 128)[4:])
    reduce_two.one()
    reduce_one.three()

    def finish(slot):
        present = jnp.where(table[T_PRESENT + slot] > 0, 1.0, 0.0)

        def rows(step, carry):
            taps = [
                cells(padded[slot, pl.ds(step * 2 + up, 2), across : across + 8])
                for up in range(3)
                for across in range(3)
            ]
            result = product(jnp.concatenate(taps, axis=1), forward[1])
            fresh = cells(state_blocks[slot, pl.ds(step * 2, 2)]).astype(F32) + result
            fresh = (fresh * present).astype(BF16)
            for half in range(2):
                part = slice(half * 128, half * 128 + 128)
                next_state[slot, step * 2 + half] = product(turns[1], fresh[part]).astype(BF16)
            return carry

        lax.fori_loop(0, 4, rows, 0)

    def close(slot):
        present = jnp.where(table[T_PRESENT + slot] > 0, 1.0, 0.0)

        def rows(step, carry):
            grad = cells(grad_blocks[slot, step])
            summed = (grad.astype(F32) + cells(total[slot, step])) * present
            cell_grad[slot, step] = product(turns[1], summed.astype(BF16)).astype(BF16)
            return carry

        lax.fori_loop(0, 8, rows, 0)

    reduce_two.two()
    reduce_one.four()
    finish(0)
    reduce_two.three()
    finish(1)
    reduce_one.five()
    reduce_two.four()
    back_one.wait()
    take_back(table, in_d, given_strips, given_corners, total)
    close(0)
    close(1)
    reduce_two.five()
    reduce_one.end(sums, 0, scale, None)
    reduce_two.end(sums, 1, scale, over)


def vmem(shape, kind):
    return pltpu.VMEM(shape, kind)


def specs(kinds):
    return [pl.BlockSpec(memory_space=pltpu.SMEM if kind == "s" else pltpu.VMEM) for kind in kinds]


def shape(dims, kind):
    return jax.ShapeDtypeStruct(dims, kind)


TILES = (2, 8, 8, 16, 128)
STRIPS = (8, 8, 16, 128)
CORNERS = (8, 16, 128)
SENT = (6, PART, 16, 128)
NATURAL = (2, 8, 128, 128)


def sum_buffers():
    return [
        vmem((2, HALF, 16, 128), BF16), vmem((HALF, 16, 128), BF16), vmem((HALF, 16, 128), BF16),
        vmem((15, CHUNK, 16, 128), BF16), vmem((8, CHUNK, 16, 128), BF16), vmem((16, CHUNK, 16, 128), BF16),
        vmem((HALF, 16, 128), BF16), vmem((HALF, 16, 128), BF16), vmem((HALF, 16, 128), F32),
    ]


def routed(cell_state, cotangent, kernels, slot_of_tile, neighbours, rotations, corner_flags):
    table = pl.pallas_call(
        plan_kernel,
        out_shape=shape((T_SIZE,), jnp.int32),
        in_specs=specs("ssss"),
        out_specs=specs("s")[0],
        scratch_shapes=[pltpu.SMEM((2 * SPAN,), jnp.int32)],
    )(slot_of_tile, neighbours, rotations, corner_flags)
    scale = 1.0 / math.sqrt(
        cell_state.shape[0] * lax.axis_size("dp") * slot_of_tile.shape[0] * cell_state.shape[2] ** 2
    )
    next_state, cell_grad, sums, over = pl.pallas_call(
        functools.partial(whole, scale),
        out_shape=[
            shape(NATURAL, BF16), shape(NATURAL, BF16), shape((2, UNITS, 16, 128), F32), shape((16, 128), F32)
        ],
        in_specs=specs("svvvv"),
        out_specs=specs("vvvv"),
        scratch_shapes=[
            vmem(TILES, BF16), vmem(TILES, BF16), vmem(TILES, BF16),
            vmem(STRIPS, BF16), vmem(CORNERS, BF16), vmem(STRIPS, BF16), vmem(CORNERS, BF16),
        ]
        + [vmem(SENT, BF16)] * 8
        + [
            vmem((2, 1152, 128), BF16), vmem((2, 1152, 128), BF16),
            vmem((2, 12, 12, 16, 128), BF16), vmem((2, 10, 10, 16, 128), F32), vmem(TILES, F32),
            vmem((2, 10, 10, 16, 128), BF16), vmem((10, 20, 16, 128), BF16), vmem((9, 20, 16, 128), BF16),
            vmem((8, 16, 16, 128), F32), vmem((10, 20, 16, 128), BF16), vmem((11, 20, 16, 128), BF16),
            vmem((128, 2048), BF16),
        ]
        + sum_buffers()
        + sum_buffers()
        + [
            pltpu.SemaphoreType.DMA((4, 2, 6)),
            pltpu.SemaphoreType.DMA((2, 39)),
            pltpu.SemaphoreType.DMA((2, 39)),
        ],
        compiler_params=pltpu.CompilerParams(
            vmem_limit_bytes=VMEM_BYTES, collective_id=1, has_side_effects=True
        ),
    )(
        table, cell_state.reshape(NATURAL), cotangent.reshape(NATURAL), kernels,
        jnp.asarray(permutations(), BF16),
    )
    done = (next_state.reshape(cell_state.shape), cell_grad.reshape(cell_state.shape), sums.reshape(kernels.shape))
    arrays = (cell_state, cotangent, kernels, slot_of_tile, neighbours, rotations, corner_flags)
    return lax.cond(over[0, 0] == 0, lambda *_: done, shards, *arrays)


def solution(mesh):
    in_specs = (
        P("dp", "space", None, None, None),
        P("dp", "space", None, None, None),
        P(),
        P(),
        P(),
        P(),
        P(),
    )
    out_specs = (P("dp", "space", None, None, None), P("dp", "space", None, None, None), P())
    return jax.shard_map(routed, mesh=mesh, in_specs=in_specs, out_specs=out_specs, check_vma=False)
```

profile of v0, /device:TPU:1, one launch (start us, length us, event | category | flops | bytes accessed | tf_op | source)
XLA Modules:
  0.0 97.4 jit_solution(11914658561357365486)
XLA Ops:
  7.2 0.0 copy-start.33
  7.2 0.0 copy-start.34
  7.2 0.0 copy-start.35
  7.2 0.0 copy-start
  7.2 0.0 copy-start.1
  7.2 0.0 copy-start.10
  7.2 0.0 copy-start.16
  7.2 1.6 %copy.487.near_ref = s32[192,8]{1,0:T(8,128)} copy(s32[192,8]{0,1:T(8,128)} %param.20) | data formatting | bytes 12288 | tf_op args[4]
  8.8 1.5 %copy.488.turn_ref = s32[192,8]{1,0:T(8,128)} copy(s32[192,8]{0,1:T(8,128)} %param.21) | data formatting | bytes 12288 | tf_op args[5]
  10.3 1.4 %copy.489.flag_ref = s32[192,4]{1,0:T(8,128)} copy(s32[192,4]{0,1:T(4,128)} %param.22) | data formatting | bytes 6144 | tf_op args[6]
  11.7 8.6 %shard_map.109.table = s32[224]{0:T(256)} custom-call(s32[192]{0:T(256)} %slot_ref.1, s32[192,8]{1,0:T(8,128)} %copy.487.near_ref, s32[192,8]{1,0:T(8,128)} %copy.488.turn_ref, s32[192,4]{1,0:T(8,128)} %copy.489.flag_ref), custom_call_target="tpu_custom_call" | custom-call | tf_op jit(solution)/shard_map/pallas_call | solution.py:911
  20.4 62.8 %shard_map.110 = (bf16[2,8,128,128]{3,2,1,0:T(8,128)(2,1)}, bf16[2,8,128,128]{3,2,1,0:T(8,128)(2,1)}, f32[2,72,16,128]{3,2,1,0:T(8,128)}, f32[16,128]{1,0:T(8,128)}) custom-call(s32[224]{0:T(256)} %shard_map.109.table, bf16[2,8,128,128]{3,2,1,0:T(8,128)(2,1)} %bitcast.578, bf16[2,8,128,128]{3,2,1,0:T(8,128)(2,1)} %bitcast.614, ...), custom_call_target="tpu_custom_call" | custom-call | tf_op jit(solution)/shard_map/pallas_call | solution.py:921
  83.2 1.2 %slice.277 = f32[1,1]{1,0:T(1,128)} slice(f32[16,128]{1,0:T(8,128)} %get-tuple-element.46), slice={[0:1], [0:1]} | slice | bytes 8 | tf_op jit(solution)/shard_map/slice | solution.py:956
  85.0 0.0 copy-done.33
  85.0 0.0 copy-done.34
  85.0 0.0 copy-done.35
  85.1 0.0 copy-done
  85.1 0.0 copy-done.1
  85.1 0.0 copy-done.10
  85.1 0.0 copy-done.16
  85.1 2.7 %conditional.1 = (f32[2,3,3,128,128]{4,3,2,1,0:T(8,128)}, bf16[1,2,32,32,128]{4,3,2,1,0:T(8,128)(2,1)S(1)}, bf16[1,2,32,32,128]{4,3,2,1,0:T(8,128)(2,1)S(1)}) conditional(s32[]{:T(128)} %bitcast.234, (s32[192]{0:T(256)S(1)}, bf16[1,2,32,32,128]{4,3,2,1,0:T(8,128)(2,1)S(1)}, s32[192,4]{0,1:T(4,128)S(1)}, s32[192,8]{0,1:T(8,128)S(1)}, ...), branch_computations={%region_0.11_spmd, %region_8.12_spmd} | conditional | flops 3982128128 | bytes 262454240 | solution.py:956
  85.4 0.0 copy-start.22
  85.4 1.6 %copy.495 = bf16[2,8,128,128]{3,0,2,1:T(2,128)(2,1)S(1)} copy(bf16[2,8,128,128]{3,2,1,0:T(8,128)(2,1)} %get-tuple-element.179) | data formatting | bytes 1048576 | tf_op jit(solution)/shard_map
  87.0 0.1 copy.523
  87.1 0.0 copy-done.22
  87.1 0.5 copy.496
  87.7 0.1 copy.525
  87.8 0.0 copy-start.23
  87.8 0.0 copy-start.24
  87.8 2.8 %copy.776 = f32[2,3,3,128,128]{4,3,2,1,0:T(8,128)} copy(f32[2,3,3,128,128]{4,3,2,1,0:T(8,128)} %get-tuple-element.554) | data formatting | bytes 2359296
  90.5 0.0 copy-done.23
  90.5 0.0 copy-done.24
Async XLA Ops:
  7.2 77.9 %copy-start.33 = (s32[192,8]{0,1:T(8,128)S(1)}, s32[192,8]{0,1:T(8,128)}, u32[]{:S(2)}) copy-start(s32[192,8]{0,1:T(8,128)} %param.20) | copy-start | bytes 18436
  7.2 77.9 %copy-start.34 = (s32[192,8]{0,1:T(8,128)S(1)}, s32[192,8]{0,1:T(8,128)}, u32[]{:S(2)}) copy-start(s32[192,8]{0,1:T(8,128)} %param.21) | copy-start | bytes 18436
  7.2 77.9 %copy-start.35 = (s32[192,4]{0,1:T(4,128)S(1)}, s32[192,4]{0,1:T(4,128)}, u32[]{:S(2)}) copy-start(s32[192,4]{0,1:T(4,128)} %param.22) | copy-start | bytes 9220
  7.2 77.9 %copy-start = (s32[192]{0:T(256)S(1)}, s32[192]{0:T(256)}, u32[]{:S(2)}) copy-start(s32[192]{0:T(256)} %slot_ref.1) | copy-start | bytes 2308
  7.2 77.9 %copy-start.1 = (bf16[1,2,32,32,128]{4,3,2,1,0:T(8,128)(2,1)S(1)}, bf16[1,2,32,32,128]{4,3,2,1,0:T(8,128)(2,1)}, u32[]{:S(2)}) copy-start(bf16[1,2,32,32,128]{4,3,2,1,0:T(8,128)(2,1)} %param.16) | copy-start | bytes 1572868
  7.2 77.9 %copy-start.10 = (bf16[1,2,32,32,128]{4,3,2,1,0:T(8,128)(2,1)S(1)}, bf16[1,2,32,32,128]{4,3,2,1,0:T(8,128)(2,1)}, u32[]{:S(2)}) copy-start(bf16[1,2,32,32,128]{4,3,2,1,0:T(8,128)(2,1)} %param.17) | copy-start | bytes 1572868
  7.2 77.9 %copy-start.16 = (bf16[2,3,3,128,128]{4,3,2,1,0:T(8,128)(2,1)S(1)}, bf16[2,3,3,128,128]{4,3,2,1,0:T(8,128)(2,1)}, u32[]{:S(2)}) copy-start(bf16[2,3,3,128,128]{4,3,2,1,0:T(8,128)(2,1)} %kernels.1) | copy-start | bytes 1769476
  85.4 1.7 %copy-start.22 = (bf16[2,8,128,128]{3,2,1,0:T(8,128)(2,1)S(1)}, bf16[2,8,128,128]{3,2,1,0:T(8,128)(2,1)}, u32[]{:S(2)}) copy-start(bf16[2,8,128,128]{3,2,1,0:T(8,128)(2,1)} %get-tuple-element.180) | copy-start | bytes 1572868 | tf_op jit(solution)/shard_map/cond
  87.8 2.8 %copy-start.23 = (bf16[1,2,32,32,128]{4,3,2,1,0:T(8,128)(2,1)}, bf16[1,2,32,32,128]{4,3,2,1,0:T(8,128)(2,1)S(1)}, u32[]{:S(2)}) copy-start(bf16[1,2,32,32,128]{4,3,2,1,0:T(8,128)(2,1)S(1)} %get-tuple-element.553) | copy-start | bytes 1572868
  87.8 2.8 %copy-start.24 = (bf16[1,2,32,32,128]{4,3,2,1,0:T(8,128)(2,1)}, bf16[1,2,32,32,128]{4,3,2,1,0:T(8,128)(2,1)S(1)}, u32[]{:S(2)}) copy-start(bf16[1,2,32,32,128]{4,3,2,1,0:T(8,128)(2,1)S(1)} %get-tuple-element.552) | copy-start | bytes 1572868
where the time goes:
time: 97.8 us; the launch traced here: 97.4 us
  Pallas kernels  71.4 us (73%)
  between operations  14.8 us (15%)
  local copies, waits for them, and re-layouts  10.8 us (11%)
    pallas_call x1, Pallas kernels, routed(): pl.pallas_call(functools.partial(whole, scale), out_shape=[shape(NATURAL,...  62.8 us
    pallas_call x1, Pallas kernels, routed(): pl.pallas_call(plan_kernel, out_shape=shape((T_SIZE,), jnp.int32), in_spe...  8.63 us
    unnamed x22, local copies, waits for them, and re-layouts  7.29 us
    another operation x2, local copies, waits for them, and re-layouts  2.18 us

commit v1 on v0

--- a/solution.py
+++ b/solution.py
@@ -216,6 +216,16 @@
     return grad_tiles + rim_back(returned)[0]
 
 
+def sum_over(value, axis):
+    count = lax.axis_size(axis)
+    step = 1
+    while step < count:
+        pairs = [(source, source ^ step) for source in range(count)]
+        value = value + lax.ppermute(value, axis, pairs)
+        step *= 2
+    return value
+
+
 def shards(cell_state, cotangent, kernels, slot_of_tile, neighbours, rotations, corner_flags):
     plan = halo_plan(slot_of_tile, neighbours, rotations, corner_flags, cell_state.shape[1])
     keep_slot = plan[3][None, :, None, None, None]
@@ -251,7 +261,7 @@
         )
         gradient = (gradient.astype(jnp.float32) + returned).astype(jnp.bfloat16)
     stacked = jnp.stack(kernel_terms)
-    stacked = lax.psum(stacked, ("space", "dp"))
+    stacked = sum_over(sum_over(stacked, "space"), "dp")
     return (next_state, gradient, stacked * norm_scale)
 
 
@@ -339,9 +349,9 @@
             row = jnp.maximum(tile, 0)
             for piece in range(8):
                 kind = piece // 4
-                source = slot_ref[near_ref[row, piece]]
+                source = slot_ref[near_ref[piece, row]]
                 hit = (tile >= 0) & (source // 2 == me)
-                entry = source % 2 * 4 + ((piece + 2 + turn_ref[row, piece]) & 3)
+                entry = source % 2 * 4 + ((piece + 2 + turn_ref[piece, row]) & 3)
                 cap = CORNER_CAP if kind else STRIP_CAP[where]
                 rank = jnp.minimum(seen[kind], cap - 1)
                 over = over + jnp.where(hit & (seen[kind] >= cap), 1, 0)
@@ -358,8 +368,8 @@
         table[T_PRESENT + slot] = valid
         for piece in range(8):
             kind = piece // 4
-            source = slot_ref[near_ref[row, piece]]
-            turn = turn_ref[row, piece] & 3
+            source = slot_ref[near_ref[piece, row]]
+            turn = turn_ref[piece, row] & 3
             offset = jnp.clip((source // 2 - me + 3 + SPAN) % SPAN, 0, 6)
             where = jnp.where(offset == 3, SELF, jnp.where(offset < 3, offset, offset - 1))
             rank = jnp.int32(0)
@@ -370,7 +380,7 @@
             rank = jnp.minimum(rank, 3 if kind else 1)
             keep = valid
             if kind:
-                keep = valid * jnp.where(flag_ref[row, piece - 4] == 0, 1, 0)
+                keep = valid * jnp.where(flag_ref[piece - 4, row] == 0, 1, 0)
             entry = source % 2 * 4 + ((piece + 2 + turn) & 3)
             base = T_PIECES + (slot * 8 + piece) * 6
             table[base] = valid
@@ -647,21 +657,49 @@
             self.pair_send[at : at + CHUNK] = self.wide_in[index]
         self.copy(self.pair_send, self.pair_in, 38, self.place.mate)
 
-    def end(self, out, layer, scale, over):
+    def end(self, out, layer, over):
         self.wait()
         core = self.place.core
-        mine, other = self.pair_send[...].astype(F32), self.pair_in[...].astype(F32)
-        out[layer, :36] = jnp.where(core == 0, mine[:36], other[:36]) * scale
-        out[layer, 36:] = jnp.where(core == 0, other[:36], mine[:36]) * scale
+        mine, other = self.pair_send[...], self.pair_in[...]
+        out[layer, :36] = jnp.where(core == 0, mine[:36], other[:36])
+        out[layer, 36:] = jnp.where(core == 0, other[:36], mine[:36])
         if over is not None:
-            over[...] = mine[36]
+            over[0] = jnp.where(jnp.max(mine[36].astype(F32)) > 0.0, 1, 0)
+
+
+def columns(value, first, count):
+    rows, wide = value.shape[:2]
+    paired = value.reshape(rows, wide // 2, 2, 16, 128)
+    return [
+        cells(paired[:, (first + step) // 2 : (first + step) // 2 + count, (first + step) % 2])
+        for step in range(4)
+    ]
+
+
+def split_pairs(result, rows, count):
+    wide = result.reshape(rows, count, 16, 256)
+    return jnp.stack([wide[..., :128], wide[..., 128:]], axis=2).reshape(rows, count * 2, 16, 128)
+
+
+def paired_conv(sources, first, count, weight):
+    taps = [tap for value in sources for tap in columns(value, first, count)]
+    result = product(jnp.concatenate(taps, axis=1), weight)
+    return split_pairs(result, sources[0].shape[0], count)
+
+
+def gradient_terms(turned, windows):
+    total = None
+    for at, taps in windows:
+        part = product(turned[:, at : at + taps[0].shape[0]], jnp.concatenate(taps, axis=1))
+        total = part if total is None else total + part
+    return [total[:, tap * 128 : tap * 128 + 128].T for tap in range(9)]
 
 
 def whole(
-    scale, table, state, cotangent, kernels, turns, next_state, cell_grad, sums, over,
+    table, state, cotangent, kernels, turns, fresh, summed, sums, over,
     state_blocks, grad_blocks, hidden_blocks, strips, corners, given_strips, given_corners,
     send_a, send_b, send_c, send_d, in_a, in_b, in_c, in_d,
-    forward, flipped, grad_wide, wide, total, padded, even, odd, before, grad_even, grad_odd, grad_turned,
+    forward, flipped, grad_wide, wide, total, padded, even, odd, slope, grad_even, grad_odd, grad_turned,
     *rest,
 ):
     sum_one, sum_two = rest[:9], rest[9:18]
@@ -697,11 +735,18 @@
     pl.semaphore_wait(barrier, 29)
     rims_one.start()
 
+    forward[...] = jnp.zeros_like(forward)
+    flipped[...] = jnp.zeros_like(flipped)
     for layer in range(2):
-        for tap in range(9):
-            weight = kernels[layer, tap // 3, tap % 3]
-            forward[layer, tap * 128 : tap * 128 + 128] = weight
-            flipped[layer, tap * 128 : tap * 128 + 128] = weight.astype(F32).T.astype(BF16)
+        for up in range(3):
+            for across in range(3):
+                weight = kernels[layer, up, across]
+                turned = weight.T
+                for side in range(2):
+                    at = (up * 4 + side + across) * 128
+                    forward[layer, at : at + 128, side * 128 : side * 128 + 128] = weight
+                    at = (up * 4 + side + 2 - across) * 128
+                    flipped[layer, at : at + 128, side * 128 : side * 128 + 128] = turned
     grad_wide[...] = jnp.zeros_like(grad_wide)
     for slot in range(2):
         present = jnp.where(table[T_PRESENT + slot] > 0, 1.0, 0.0)
@@ -710,18 +755,9 @@
             grad_blocks[slot, row] = moved
             grad_wide[slot, 2 + row, 2:10] = moved
     for slot in range(2):
-
-        def rows_back(step, carry):
-            taps = [
-                cells(grad_wide[slot, pl.ds(step * 2 + 2 - up, 2), 2 - across : 12 - across])
-                for up in range(3)
-                for across in range(3)
-            ]
-            result = product(jnp.concatenate(taps, axis=1), flipped[1])
-            wide[slot, pl.ds(step * 2, 2)] = result.reshape(2, 10, 16, 128)
-            return carry
-
-        lax.fori_loop(0, 5, rows_back, 0)
+        for row in (0, 5):
+            sources = [grad_wide[slot, row + 2 - up : row + 7 - up] for up in range(3)]
+            wide[slot, row : row + 5] = paired_conv(sources, 0, 5, flipped[1])
         total[slot] = wide[slot, 1:9, 1:9]
     give_back(table, wide, turns, send_b, given_strips, given_corners)
     back_two.start()
@@ -737,41 +773,27 @@
             for slot in range(2)
         ]
         odd[row] = jnp.concatenate(both, axis=1).astype(BF16)
-
-    def window(row, up, across, count):
-        source, at = ((odd, row), (even, row + 1), (odd, row + 1))[up]
-        return cells(source[pl.ds(at, count), 1 + across : 17 + across])
-
-    def first(row, carry):
-        taps = [window(row, up, across, 1) for up in range(3) for across in range(3)]
-        result = product(jnp.concatenate(taps, axis=1), forward[0]).reshape(16, 16, 128)
-        before[row] = result
-        hidden = gelu_parts(result)[0]
+    for row in (0, 4):
+        sources = [odd[row : row + 4], even[row + 1 : row + 5], odd[row + 1 : row + 5]]
+        result = paired_conv(sources, 1, 8, forward[0])
+        hidden, slopes = gelu_parts(result)
+        slope[row : row + 4] = slopes
         for slot in range(2):
-            part = hidden[:, slot * 8 : slot * 8 + 8].reshape(8, 16, 128)
-            hidden_blocks[slot, row] = part.astype(BF16)
-        return carry
-
-    lax.fori_loop(0, 8, first, 0)
+            part = hidden[:, :, slot * 8 : slot * 8 + 8].reshape(4, 8, 16, 128)
+            hidden_blocks[slot, row : row + 4] = part.astype(BF16)
     take_rims(hidden_blocks, strips, corners)
     send_rims(table, strips, corners, send_c)
     rims_two.start()
 
+    grad_even[...] = jnp.zeros_like(grad_even)
+    grad_odd[...] = jnp.zeros_like(grad_odd)
     back_two.wait()
     take_back(table, in_b, given_strips, given_corners, total)
-    grad_even[...] = jnp.zeros_like(grad_even)
-    grad_odd[...] = jnp.zeros_like(grad_odd)
-
-    def pointwise(row, carry):
+    for row in range(8):
         both = [total[slot, row].astype(BF16).astype(F32).reshape(16, 8, 128) for slot in range(2)]
-        grad = jnp.concatenate(both, axis=1) * gelu_parts(before[row])[1]
-        grad = grad.astype(BF16)
+        grad = (jnp.concatenate(both, axis=1) * slope[row]).astype(BF16)
         grad_even[row + 1, 2:18] = grad
-        at = pl.multiple_of(row * 256, 256)
-        grad_turned[:, pl.ds(at, 256)] = cells(grad).astype(F32).T.astype(BF16)
-        return carry
-
-    lax.fori_loop(0, 8, pointwise, 0)
+        grad_turned[:, row * 256 : row * 256 + 256] = cells(grad).T
     for row in range(9):
         low = grad_even[row, 2:18].astype(F32)
         high = grad_even[row + 1, 2:18].astype(F32)
@@ -780,31 +802,28 @@
             for slot in range(2)
         ]
         grad_odd[row + 1, 2:18] = jnp.concatenate(both, axis=1).astype(BF16)
-
-    def returned(row, carry):
-        taps = []
-        for up in range(3):
-            source, at = ((grad_odd, row + 1), (grad_even, row), (grad_odd, row))[up]
-            for across in range(3):
-                taps.append(cells(source[at, 2 - across : 20 - across]))
-        result = product(jnp.concatenate(taps, axis=1), flipped[0]).reshape(18, 16, 128)
-        blank = jnp.zeros((1, 8, 128), F32)
+    for row in (0, 5):
+        sources = [grad_odd[row + 1 : row + 6], grad_even[row : row + 5], grad_odd[row : row + 5]]
+        result = paired_conv(sources, 0, 9, flipped[0])
+        blank = jnp.zeros((5, 1, 8, 128), F32)
         for slot in range(2):
-            part = jnp.concatenate([blank, result[:, slot * 8 : slot * 8 + 8], blank], axis=0)
-            wide[slot, row] = part.reshape(10, 16, 128)
-        return carry
-
-    lax.fori_loop(0, 10, returned, 0)
+            part = jnp.concatenate([blank, result[:, :, slot * 8 : slot * 8 + 8], blank], axis=1)
+            wide[slot, row : row + 5] = part.reshape(5, 10, 16, 128)
     give_back(table, wide, turns, send_d, given_strips, given_corners)
     back_one.start()
     for slot in range(2):
         total[slot] = wide[slot, 1:9, 1:9]
 
-    for up in range(3):
-        for across in range(3):
-            term = product(grad_turned[...], window(0, up, across, 8))
-            reduce_one.put((up * 3 + across) * 8, term.T.reshape(8, 16, 128)[:4])
-            reduce_one.put((up * 3 + across) * 8 + 4, term.T.reshape(8, 16, 128)[4:])
+    windows = []
+    for row in range(0, 8, 2):
+        taps = []
+        for source, at in ((odd, row), (even, row + 1), (odd, row + 1)):
+            for across in range(3):
+                taps.append(cells(source[at : at + 2, 1 + across : 17 + across]))
+        windows.append((row * 256, taps))
+    for tap, term in enumerate(gradient_terms(grad_turned, windows)):
+        reduce_one.put(tap * 8, blocks(term)[:4])
+        reduce_one.put(tap * 8 + 4, blocks(term)[4:])
     blank = jnp.zeros((1, 16, 128), F32)
     broken = blank + table[T_OVER].astype(F32)
     for half in range(2):
@@ -812,57 +831,35 @@
         reduce_two.half_send[half, 36:37] = broken.astype(BF16)
     reduce_one.one()
 
+    for slot in range(2):
+        for step in range(4):
+            at = slot * 1024 + step * 256
+            grad_turned[:, at : at + 256] = cells(grad_blocks[slot, step * 2 : step * 2 + 2]).T
     rims_two.wait()
     widen(table, hidden_blocks, strips, corners, in_c, turns, padded)
-    for slot in range(2):
-        for step in range(4):
-            grad = cells(grad_blocks[slot, step * 2 : step * 2 + 2])
-            at = slot * 1024 + step * 256
-            grad_turned[:, at : at + 256] = grad.astype(F32).T.astype(BF16)
     reduce_one.two()
-    for up in range(3):
-        for across in range(3):
-            term = sum(
-                product(
-                    grad_turned[:, slot * 1024 : slot * 1024 + 1024],
-                    cells(padded[slot, up : up + 8, across : across + 8]),
-                )
-                for slot in range(2)
-            )
-            reduce_two.put((up * 3 + across) * 8, term.T.reshape(8, 16, 128)[:4])
-            reduce_two.put((up * 3 + across) * 8 + 4, term.T.reshape(8, 16, 128)[4:])
-    reduce_two.one()
-    reduce_one.three()
-
-    def finish(slot):
-        present = jnp.where(table[T_PRESENT + slot] > 0, 1.0, 0.0)
-
-        def rows(step, carry):
+    windows = []
+    for slot in range(2):
+        for row in (0, 4):
             taps = [
-                cells(padded[slot, pl.ds(step * 2 + up, 2), across : across + 8])
+                cells(padded[slot, row + up : row + up + 4, across : across + 8])
                 for up in range(3)
                 for across in range(3)
             ]
-            result = product(jnp.concatenate(taps, axis=1), forward[1])
-            fresh = cells(state_blocks[slot, pl.ds(step * 2, 2)]).astype(F32) + result
-            fresh = (fresh * present).astype(BF16)
-            for half in range(2):
-                part = slice(half * 128, half * 128 + 128)
-                next_state[slot, step * 2 + half] = product(turns[1], fresh[part]).astype(BF16)
-            return carry
-
-        lax.fori_loop(0, 4, rows, 0)
-
-    def close(slot):
+            windows.append((slot * 1024 + row * 128, taps))
+    for tap, term in enumerate(gradient_terms(grad_turned, windows)):
+        reduce_two.put(tap * 8, blocks(term)[:4])
+        reduce_two.put(tap * 8 + 4, blocks(term)[4:])
+    reduce_two.one()
+    reduce_one.three()
+
+    def finish(slot):
         present = jnp.where(table[T_PRESENT + slot] > 0, 1.0, 0.0)
-
-        def rows(step, carry):
-            grad = cells(grad_blocks[slot, step])
-            summed = (grad.astype(F32) + cells(total[slot, step])) * present
-            cell_grad[slot, step] = product(turns[1], summed.astype(BF16)).astype(BF16)
-            return carry
-
-        lax.fori_loop(0, 8, rows, 0)
+        for row in (0, 4):
+            sources = [padded[slot, row + up : row + up + 4] for up in range(3)]
+            result = paired_conv(sources, 0, 4, forward[1])
+            value = state_blocks[slot, row : row + 4].astype(F32) + result
+            fresh[slot, row : row + 4] = (value * present).astype(BF16)
 
     reduce_two.two()
     reduce_one.four()
@@ -873,11 +870,20 @@
     reduce_two.four()
     back_one.wait()
     take_back(table, in_d, given_strips, given_corners, total)
-    close(0)
-    close(1)
+    for slot in range(2):
+        present = jnp.where(table[T_PRESENT + slot] > 0, 1.0, 0.0)
+        value = grad_blocks[slot].astype(F32) + total[slot]
+        summed[slot] = (value * present).astype(BF16)
     reduce_two.five()
-    reduce_one.end(sums, 0, scale, None)
-    reduce_two.end(sums, 1, scale, over)
+    reduce_one.end(sums, 0, None)
+    reduce_two.end(sums, 1, over)
+
+
+def settle(scale, fresh, summed, sums, back, next_state, cell_grad, kernel_grads):
+    for row in range(fresh.shape[0]):
+        next_state[row] = product(back[...], cells(fresh[row])).astype(BF16)
+        cell_grad[row] = product(back[...], cells(summed[row])).astype(BF16)
+    kernel_grads[...] = sums[...].astype(F32) * scale
 
 
 def vmem(shape, kind):
@@ -905,6 +911,27 @@
         vmem((15, CHUNK, 16, 128), BF16), vmem((8, CHUNK, 16, 128), BF16), vmem((16, CHUNK, 16, 128), BF16),
         vmem((HALF, 16, 128), BF16), vmem((HALF, 16, 128), BF16), vmem((HALF, 16, 128), F32),
     ]
+
+
+def finished(scale, fresh, summed, sums, back):
+    def rows(count, *tail):
+        return pl.BlockSpec((count,) + tail, lambda step: (step,) + (0,) * len(tail))
+
+    return pl.pallas_call(
+        functools.partial(settle, scale),
+        grid=(4,),
+        out_shape=[
+            shape((16, 128, 128), BF16), shape((16, 128, 128), BF16), shape((2 * UNITS, 16, 128), F32)
+        ],
+        in_specs=[
+            rows(4, 8, 16, 128), rows(4, 8, 16, 128), rows(36, 16, 128),
+            pl.BlockSpec((128, 128), lambda step: (0, 0)),
+        ],
+        out_specs=[rows(4, 128, 128), rows(4, 128, 128), rows(36, 16, 128)],
+    )(
+        fresh.reshape(16, 8, 16, 128), summed.reshape(16, 8, 16, 128),
+        sums.reshape(2 * UNITS, 16, 128), back,
+    )
 
 
 def routed(cell_state, cotangent, kernels, slot_of_tile, neighbours, rotations, corner_flags):
@@ -914,24 +941,25 @@
         in_specs=specs("ssss"),
         out_specs=specs("s")[0],
         scratch_shapes=[pltpu.SMEM((2 * SPAN,), jnp.int32)],
-    )(slot_of_tile, neighbours, rotations, corner_flags)
+    )(slot_of_tile, neighbours.T, rotations.T, corner_flags.T)
     scale = 1.0 / math.sqrt(
         cell_state.shape[0] * lax.axis_size("dp") * slot_of_tile.shape[0] * cell_state.shape[2] ** 2
     )
-    next_state, cell_grad, sums, over = pl.pallas_call(
-        functools.partial(whole, scale),
+    turns = permutations()
+    fresh, summed, sums, over = pl.pallas_call(
+        whole,
         out_shape=[
-            shape(NATURAL, BF16), shape(NATURAL, BF16), shape((2, UNITS, 16, 128), F32), shape((16, 128), F32)
+            shape(TILES, BF16), shape(TILES, BF16), shape((2, UNITS, 16, 128), BF16), shape((1,), jnp.int32)
         ],
         in_specs=specs("svvvv"),
-        out_specs=specs("vvvv"),
+        out_specs=specs("vvvs"),
         scratch_shapes=[
             vmem(TILES, BF16), vmem(TILES, BF16), vmem(TILES, BF16),
             vmem(STRIPS, BF16), vmem(CORNERS, BF16), vmem(STRIPS, BF16), vmem(CORNERS, BF16),
         ]
         + [vmem(SENT, BF16)] * 8
         + [
-            vmem((2, 1152, 128), BF16), vmem((2, 1152, 128), BF16),
+            vmem((2, 1536, 256), BF16), vmem((2, 1536, 256), BF16),
             vmem((2, 12, 12, 16, 128), BF16), vmem((2, 10, 10, 16, 128), F32), vmem(TILES, F32),
             vmem((2, 10, 10, 16, 128), BF16), vmem((10, 20, 16, 128), BF16), vmem((9, 20, 16, 128), BF16),
             vmem((8, 16, 16, 128), F32), vmem((10, 20, 16, 128), BF16), vmem((11, 20, 16, 128), BF16),
@@ -949,11 +977,16 @@
         ),
     )(
         table, cell_state.reshape(NATURAL), cotangent.reshape(NATURAL), kernels,
-        jnp.asarray(permutations(), BF16),
-    )
-    done = (next_state.reshape(cell_state.shape), cell_grad.reshape(cell_state.shape), sums.reshape(kernels.shape))
+        jnp.asarray(turns, BF16),
+    )
+    back = jnp.asarray(turns[1], BF16)
     arrays = (cell_state, cotangent, kernels, slot_of_tile, neighbours, rotations, corner_flags)
-    return lax.cond(over[0, 0] == 0, lambda *_: done, shards, *arrays)
+
+    def fast(*_):
+        outs = finished(scale, fresh, summed, sums, back)
+        return tuple(out.reshape(like) for out, like in zip(outs, (cell_state.shape, cell_state.shape, kernels.shape)))
+
+    return lax.cond(over[0] == 0, fast, shards, *arrays)
 
 
 def solution(mesh):

time: 97.8 us -> 68.7 us (0.70)
  between operations: 14.8 us -> 1.4 us
  local copies, waits for them, and re-layouts: 10.8 us -> 1.37 us
  Pallas kernels: 71.4 us -> 65.4 us
    unnamed x22 -> x20, local copies, waits for them, and re-layouts: 7.29 us -> 1.37 us
    pallas_call x1, Pallas kernels: 8.63 us -> 4.3 us  [routed(): pl.pallas_call(plan_kernel, out_shape=shape((T_SIZE,), jnp.int32), in_spe...]
    another operation x2 -> x0, local copies, waits for them, and re-layouts: 2.18 us -> none
    pallas_call x1 -> x2, Pallas kernels: 62.8 us -> 61.1 us  [the longest x1 58.3 us: routed(): pl.pallas_call(whole, out_shape=[shape(TILES, BF16), shape(TILES, BF16),...]
    slice x1 -> x0, local copies, waits for them, and re-layouts: 1.19 us -> none  [routed(): return lax.cond(over[0, 0] == 0, lambda *_: done, shards, *arrays)]
where the time goes in v1:
time: 68.7 us; the launch traced here: 68.5 us
  Pallas kernels  65.4 us (95%)
  between operations  1.4 us (2%)
  local copies, waits for them, and re-layouts  1.37 us (2%)
    pallas_call x1, Pallas kernels, routed(): pl.pallas_call(whole, out_shape=[shape(TILES, BF16), shape(TILES, BF16),...  58.3 us
    pallas_call x1, Pallas kernels, routed(): pl.pallas_call(plan_kernel, out_shape=shape((T_SIZE,), jnp.int32), in_spe...  4.3 us
    pallas_call x1, Pallas kernels, finished(): pl.pallas_call(functools.partial(settle, scale), grid=(4,), out_shape=[sh...  2.88 us

profile of v1, /device:TPU:1, one launch (start us, length us, event | category | flops | bytes accessed | tf_op | source)
XLA Modules:
  0.0 68.5 jit_solution(13197114863335942668)
XLA Ops:
  0.6 0.0 copy-start.33
  0.6 0.0 copy-start.34
  0.7 0.0 copy-start.35
  0.7 0.0 copy-start
  0.7 0.0 copy-start.1
  0.7 0.0 copy-start.6
  0.7 0.0 copy-start.14
  0.7 4.3 %shard_map.119.table = s32[224]{0:T(256)} custom-call(s32[192]{0:T(256)} %slot_ref.1, s32[8,192]{1,0:T(8,128)} %bitcast.683, s32[8,192]{1,0:T(8,128)} %bitcast.684, s32[4,192]{1,0:T(4,128)} %bitcast.686), custom_call_target="tpu_custom_call" | custom-call | tf_op jit(solution)/shard_map/pallas_call | solution.py:938
  5.0 58.3 %shard_map.120 = (bf16[2,8,8,16,128]{4,3,2,1,0:T(8,128)(2,1)}, bf16[2,8,8,16,128]{4,3,2,1,0:T(8,128)(2,1)}, bf16[2,72,16,128]{3,2,1,0:T(8,128)(2,1)}, s32[1]{0:T(128)}) custom-call(s32[224]{0:T(256)} %shard_map.119.table, bf16[2,8,128,128]{3,2,1,0:T(8,128)(2,1)} %bitcast.584, bf16[2,8,128,128]{3,2,1,0:T(8,128)(2,1)} %bitcast.626, ...), custom_call_target="tpu_custom_call" | custom-call | tf_op jit(solution)/shard_map/pallas_call | solution.py:949
  63.9 0.0 copy-done.33
  63.9 0.0 copy-done.34
  63.9 0.0 copy-done.35
  63.9 0.0 copy-done
  63.9 0.0 copy-done.1
  63.9 0.0 copy-done.6
  64.0 0.0 copy-done.14
  64.0 3.2 %conditional.1 = (f32[2,3,3,128,128]{4,3,2,1,0:T(8,128)S(1)}, bf16[1,2,32,32,128]{4,3,2,1,0:T(8,128)(2,1)S(1)}, bf16[1,2,32,32,128]{4,3,2,1,0:T(8,128)(2,1)S(1)}) conditional(s32[]{:T(128)} %bitcast.240, (s32[192]{0:T(256)S(1)}, bf16[1,2,32,32,128]{4,3,2,1,0:T(8,128)(2,1)S(1)}, s32[192,4]{0,1:T(4,128)S(1)}, s32[192,8]{0,1:T(8,128)S(1)}, ...), branch_computations={%region_0.10_spmd, %region_7.11_spmd} | conditional | flops 3985077248 | bytes 308919744 | solution.py:989
  64.2 2.9 %branch_1_fun.1 = (bf16[16,128,128]{2,1,0:T(8,128)(2,1)S(1)}, bf16[16,128,128]{2,1,0:T(8,128)(2,1)S(1)}, f32[144,16,128]{2,1,0:T(8,128)S(1)}) custom-call(bf16[16,8,16,128]{3,2,1,0:T(8,128)(2,1)} %bitcast.647, bf16[16,8,16,128]{3,2,1,0:T(8,128)(2,1)} %bitcast.648, bf16[144,16,128]{2,1,0:T(8,128)(2,1)} %bitcast.646, bf16[128,128]{1,0:T(8,128)(2,1)} %constant.169.clone.1.back), custom_call_target="tpu_custom_call" | custom-call | tf_op jit(solution)/shard_map/cond/branch_1_fun/pallas_call | solution.py:920
  67.1 0.0 copy-start.11
  67.1 0.0 copy-start.18
  67.2 0.0 copy-start.19
  67.2 1.0 %copy-done.11 = f32[2,3,3,128,128]{4,3,2,1,0:T(8,128)} copy-done((f32[2,3,3,128,128]{4,3,2,1,0:T(8,128)}, f32[2,3,3,128,128]{4,3,2,1,0:T(8,128)S(1)}, u32[]{:S(2)}) %copy-start.11) | copy-done | bytes 1179672
  68.1 0.2 copy-done.18
  68.3 0.2 copy-done.19
Async XLA Ops:
  0.6 63.3 %copy-start.33 = (s32[192,8]{0,1:T(8,128)S(1)}, s32[192,8]{0,1:T(8,128)}, u32[]{:S(2)}) copy-start(s32[192,8]{0,1:T(8,128)} %param.21) | copy-start | bytes 18436
  0.6 63.3 %copy-start.34 = (s32[192,8]{0,1:T(8,128)S(1)}, s32[192,8]{0,1:T(8,128)}, u32[]{:S(2)}) copy-start(s32[192,8]{0,1:T(8,128)} %param.22) | copy-start | bytes 18436
  0.7 63.3 %copy-start.35 = (s32[192,4]{0,1:T(4,128)S(1)}, s32[192,4]{0,1:T(4,128)}, u32[]{:S(2)}) copy-start(s32[192,4]{0,1:T(4,128)} %param.23) | copy-start | bytes 9220
  0.7 63.3 %copy-start = (s32[192]{0:T(256)S(1)}, s32[192]{0:T(256)}, u32[]{:S(2)}) copy-start(s32[192]{0:T(256)} %slot_ref.1) | copy-start | bytes 2308
  0.7 63.3 %copy-start.1 = (bf16[1,2,32,32,128]{4,3,2,1,0:T(8,128)(2,1)S(1)}, bf16[1,2,32,32,128]{4,3,2,1,0:T(8,128)(2,1)}, u32[]{:S(2)}) copy-start(bf16[1,2,32,32,128]{4,3,2,1,0:T(8,128)(2,1)} %param.17) | copy-start | bytes 1572868
  0.7 63.3 %copy-start.6 = (bf16[1,2,32,32,128]{4,3,2,1,0:T(8,128)(2,1)S(1)}, bf16[1,2,32,32,128]{4,3,2,1,0:T(8,128)(2,1)}, u32[]{:S(2)}) copy-start(bf16[1,2,32,32,128]{4,3,2,1,0:T(8,128)(2,1)} %param.18) | copy-start | bytes 1572868
  0.7 63.3 %copy-start.14 = (bf16[2,3,3,128,128]{4,3,2,1,0:T(8,128)(2,1)S(1)}, bf16[2,3,3,128,128]{4,3,2,1,0:T(8,128)(2,1)}, u32[]{:S(2)}) copy-start(bf16[2,3,3,128,128]{4,3,2,1,0:T(8,128)(2,1)} %kernels.1) | copy-start | bytes 1769476
  67.1 1.0 %copy-start.11 = (f32[2,3,3,128,128]{4,3,2,1,0:T(8,128)}, f32[2,3,3,128,128]{4,3,2,1,0:T(8,128)S(1)}, u32[]{:S(2)}) copy-start(f32[2,3,3,128,128]{4,3,2,1,0:T(8,128)S(1)} %get-tuple-element.186) | copy-start | bytes 3538948
  67.1 1.2 %copy-start.18 = (bf16[1,2,32,32,128]{4,3,2,1,0:T(8,128)(2,1)}, bf16[1,2,32,32,128]{4,3,2,1,0:T(8,128)(2,1)S(1)}, u32[]{:S(2)}) copy-start(bf16[1,2,32,32,128]{4,3,2,1,0:T(8,128)(2,1)S(1)} %get-tuple-element.188) | copy-start | bytes 1572868
  67.2 1.3 %copy-start.19 = (bf16[1,2,32,32,128]{4,3,2,1,0:T(8,128)(2,1)}, bf16[1,2,32,32,128]{4,3,2,1,0:T(8,128)(2,1)S(1)}, u32[]{:S(2)}) copy-start(bf16[1,2,32,32,128]{4,3,2,1,0:T(8,128)(2,1)S(1)} %get-tuple-element.187) | copy-start | bytes 1572868

commit v2 on v1

--- a/solution.py
+++ b/solution.py
@@ -273,10 +273,10 @@
 OFFSETS = (-3, -2, -1, 1, 2, 3)
 ORDER = (2, 3, 1, 4, 0, 5)
 SELF = 6
-NOT_STRIP, NOT_CORNER = 20, 32
+NOT_THERE = 32
 T_STRIP_LIST, T_CORNER_LIST, T_GIVE_STRIP, T_GIVE_CORNER = 0, 12, 36, 48
-T_ADD_STRIP, T_ADD_CORNER, T_PIECES, T_PRESENT = 72, 88, 104, 200
-T_OVER, T_SPARE, T_COUNT, T_SIZE = 202, 203, 208, 224
+T_ADD, T_PIECES, T_PRESENT = 72, 104, 200
+T_OVER, T_SPARE, T_SIZE = 202, 203, 208
 VMEM_BYTES = 56 * 1024 * 1024
 F32 = jnp.float32
 BF16 = jnp.bfloat16
@@ -319,9 +319,9 @@
     me = lax.axis_index("space")
     for entry in range(T_SIZE):
         table[entry] = 0
-    for entry in range(16):
-        table[T_ADD_STRIP + entry] = NOT_STRIP
-        table[T_ADD_CORNER + entry] = NOT_CORNER
+    for entry in range(8):
+        table[T_ADD + entry] = NOT_THERE
+        table[T_ADD + 16 + entry] = NOT_THERE
     for rel in range(14):
         tile_at[(me + rel // 2 - 3 + SPAN) % SPAN * 2 + rel % 2] = -1
 
@@ -333,14 +333,14 @@
 
     lax.fori_loop(0, slot_ref.shape[0] // 16, place, 0)
     over = jnp.int32(0)
-
-    def contribute(hit, kind, entry, code):
-        counter = T_COUNT + kind * 8 + entry
-        count = table[counter]
-        table[jnp.where(hit, counter, T_SPARE)] = count + 1
-        place_at = (T_ADD_CORNER if kind else T_ADD_STRIP) + entry * 2 + jnp.minimum(count, 1)
-        table[jnp.where(hit, place_at, T_SPARE)] = code
-        return jnp.where(hit & (count > 1), 1, 0)
+    core = me % 2
+
+    def contribute(hit, kind, entry, code, turn):
+        place_at = jnp.where(hit, T_ADD + kind * 16 + entry, T_SPARE)
+        taken = jnp.where(hit & (table[place_at] != NOT_THERE), 1, 0)
+        table[place_at] = code
+        table[place_at + jnp.where(hit, 8, 0)] = jnp.where(hit, turn, code)
+        return taken
 
     for where, offset in enumerate(OFFSETS):
         seen = [jnp.int32(0), jnp.int32(0)]
@@ -351,15 +351,18 @@
                 kind = piece // 4
                 source = slot_ref[near_ref[piece, row]]
                 hit = (tile >= 0) & (source // 2 == me)
-                entry = source % 2 * 4 + ((piece + 2 + turn_ref[piece, row]) & 3)
+                turn = turn_ref[piece, row] & 3
+                entry = source % 2 * 4 + ((piece + 2 + turn) & 3)
                 cap = CORNER_CAP if kind else STRIP_CAP[where]
                 rank = jnp.minimum(seen[kind], cap - 1)
+                if offset in (-3, 3):
+                    over = over + jnp.where(hit & (core == (0 if offset < 0 else 1)), 1, 0)
                 over = over + jnp.where(hit & (seen[kind] >= cap), 1, 0)
                 seen[kind] = seen[kind] + jnp.where(hit, 1, 0)
                 width = 4 if kind else 2
                 place_at = (T_CORNER_LIST if kind else T_STRIP_LIST) + where * width + rank
                 table[jnp.where(hit, place_at, T_SPARE)] = entry
-                over = over + contribute(hit, kind, entry, where * width + rank)
+                over = over + contribute(hit, kind, entry, where * width + rank, turn)
     seen = [[jnp.int32(0)] * 7, [jnp.int32(0)] * 7]
     for slot in range(2):
         tile = tile_at[me * 2 + slot]
@@ -394,7 +397,7 @@
             away = (valid > 0) & (where != SELF)
             place_at = (T_GIVE_CORNER if kind else T_GIVE_STRIP) + where * (4 if kind else 2) + rank
             table[jnp.where(away, place_at, T_SPARE)] = mine
-            over = over + contribute(own, kind, entry, (24 if kind else 12) + mine)
+            over = over + contribute(own, kind, entry, (24 if kind else 12) + mine, turn)
     table[T_OVER] = over
 
 
@@ -485,31 +488,82 @@
     send_rims(table, strips, corners, send, T_GIVE_STRIP, T_GIVE_CORNER)
 
 
+def owner_of(table, kind, entry):
+    code = table[T_ADD + kind * 16 + entry]
+    turn = table[T_ADD + kind * 16 + 8 + entry]
+    return code, turn, (entry % 4 - 2 - turn) & 3
+
+
+def copied_strip(code, arrived, strips):
+    far = jnp.minimum(code, 11)
+    near = jnp.clip(code - 12, 0, 7)
+    part = jnp.where(code < 12, arrived[far // 2, pl.ds(4 + far % 2 * 8, 8)], strips[near])
+    return jnp.where(code == NOT_THERE, jnp.zeros_like(part), part)
+
+
+def copied_corner(code, arrived, corners):
+    far = jnp.minimum(code, 23)
+    near = jnp.clip(code - 24, 0, 7)
+    part = jnp.where(code < 24, arrived[far // 4, far % 4], corners[near])
+    return jnp.where(code == NOT_THERE, jnp.zeros_like(part), part)
+
+
 def take_back(table, arrived, strips, corners, total):
     for slot in range(2):
         for side in range(4):
             at = (slot,) + EDGE_OF[side]
-            value = total[at]
-            for extra in range(2):
-                code = table[T_ADD_STRIP + (slot * 4 + side) * 2 + extra]
-                far = jnp.minimum(code, 11)
-                near = jnp.clip(code - 12, 0, 7)
-                part = jnp.where(code < 12, arrived[far // 2, pl.ds(4 + far % 2 * 8, 8)], strips[near])
-                part = jnp.where(code == NOT_STRIP, jnp.zeros_like(part), part)
-                value = value + part.astype(F32)
-            total[at] = value
+            code = owner_of(table, 0, slot * 4 + side)[0]
+            total[at] = total[at] + copied_strip(code, arrived, strips).astype(F32)
     for slot in range(2):
         for side in range(4):
             at = (slot,) + CORNER_OF[side]
-            value = total[at]
-            for extra in range(2):
-                code = table[T_ADD_CORNER + (slot * 4 + side) * 2 + extra]
-                far = jnp.minimum(code, 23)
-                near = jnp.clip(code - 24, 0, 7)
-                part = jnp.where(code < 24, arrived[far // 4, far % 4], corners[near])
-                part = jnp.where(code == NOT_CORNER, jnp.zeros_like(part), part)
-                value = value + part.astype(F32)
-            total[at] = value
+            code = owner_of(table, 1, slot * 4 + side)[0]
+            total[at] = total[at] + copied_corner(code, arrived, corners).astype(F32)
+
+
+STRIP_TAPS = (
+    ((0, 0), (0, 1), (0, 2)),
+    ((0, 2), (1, 2), (2, 2)),
+    ((2, 0), (2, 1), (2, 2)),
+    ((0, 0), (1, 0), (2, 0)),
+)
+CORNER_TAPS = ((0, 2), (2, 2), (2, 0), (0, 0))
+
+
+def rim_terms(table, arrived, given_strips, given_corners, strips, corners, turns, masked):
+    rims = []
+    for entry in range(8):
+        code, turn, edge = owner_of(table, 0, entry)
+        grad = cells(copied_strip(code, arrived, given_strips)).T
+        for choice in range(4):
+            chosen = jnp.where(edge == choice, grad, jnp.zeros_like(grad))
+            masked[choice * 128 : choice * 128 + 128, entry * 128 : entry * 128 + 128] = chosen
+        band = product(turns[turn_matrix(turn, flips(edge, turn))], cells(strips[entry])).astype(BF16)
+        blank = jnp.zeros((16, 128), BF16)
+        longer = jnp.concatenate([blank, band, blank], axis=0)
+        rims.append(jnp.concatenate([longer[step * 16 : step * 16 + 128] for step in range(3)], axis=1))
+    edges = product(masked[...], jnp.concatenate(rims, axis=0))
+    lane = lax.broadcasted_iota(jnp.int32, (128, 128), 1) // 16
+    which = jnp.zeros((128, 128), jnp.int32)
+    grads, parts = [], []
+    for entry in range(8):
+        code, turn, side = owner_of(table, 1, entry)
+        grads.append(copied_corner(code, arrived, given_corners))
+        which = jnp.where(lane == entry, side, which)
+        parts.append(turns[turn_matrix(turn, 0)][entry * 16 : entry * 16 + 16])
+    block = product(jnp.concatenate(parts, axis=0), cells(corners[...])).astype(BF16)
+    grad = jnp.concatenate(grads, axis=0).astype(F32).T
+    spread = [jnp.where(which == choice, grad, jnp.zeros_like(grad)) for choice in range(4)]
+    ends = product(jnp.concatenate(spread, axis=0).astype(BF16), block)
+    sums = [None] * 9
+    for choice in range(4):
+        rows = slice(choice * 128, choice * 128 + 128)
+        found = [(tap, edges[rows, step * 128 : step * 128 + 128]) for step, tap in enumerate(STRIP_TAPS[choice])]
+        found.append((CORNER_TAPS[choice], ends[rows]))
+        for (up, across), value in found:
+            old = sums[up * 3 + across]
+            sums[up * 3 + across] = value if old is None else old + value
+    return sums
 
 
 def halves(value):
@@ -542,16 +596,20 @@
 
 class Swap:
     def __init__(self, me, send, arrived, sems):
+        core = me % 2
+        far = 5 - 5 * core
         self.copies = []
-        for where in ORDER:
-            size = 4 + 8 * STRIP_CAP[where]
+        for where in (2, 3, 1, 4, far):
+            near = isinstance(where, int)
+            size = 4 + 8 * (STRIP_CAP[where] if near else STRIP_CAP[0])
+            offset = OFFSETS[where] if near else 3 - 6 * core
             self.copies.append(
                 pltpu.make_async_remote_copy(
                     src_ref=send.at[where, pl.ds(0, size)],
                     dst_ref=arrived.at[5 - where, pl.ds(0, size)],
-                    send_sem=sems.at[0, where],
-                    recv_sem=sems.at[1, 5 - where],
-                    device_id={"space": lax.rem(me + OFFSETS[where] + SPAN, SPAN)},
+                    send_sem=sems.at[0, where if near else 0],
+                    recv_sem=sems.at[1, 5 - where if near else 0],
+                    device_id={"space": lax.rem(me + offset + SPAN, SPAN)},
                     device_id_type=MESH_ID,
                 )
             )
@@ -603,10 +661,12 @@
         one.start()
         self.copies.append(one)
 
-    def put(self, index, value):
-        half, at = index // 36, index % 36
-        size = value.shape[0]
-        self.half_send[half, at : at + size] = value.astype(BF16)
+    def put(self, terms):
+        for tap, term in enumerate(terms):
+            value = blocks(term.astype(BF16))
+            for part in range(2):
+                half, at = divmod(tap * 8 + part * 4, 36)
+                self.half_send[half, at : at + 4] = value[part * 4 : part * 4 + 4]
 
     def wait(self):
         for one in self.copies:
@@ -687,22 +747,25 @@
     return split_pairs(result, sources[0].shape[0], count)
 
 
-def gradient_terms(turned, windows):
+def gradient_terms(turned, windows, extra=None):
     total = None
     for at, taps in windows:
         part = product(turned[:, at : at + taps[0].shape[0]], jnp.concatenate(taps, axis=1))
         total = part if total is None else total + part
-    return [total[:, tap * 128 : tap * 128 + 128].T for tap in range(9)]
+    terms = [total[:, tap * 128 : tap * 128 + 128] for tap in range(9)]
+    if extra is not None:
+        terms = [term if more is None else term + more for term, more in zip(terms, extra)]
+    return [term.T for term in terms]
 
 
 def whole(
     table, state, cotangent, kernels, turns, fresh, summed, sums, over,
     state_blocks, grad_blocks, hidden_blocks, strips, corners, given_strips, given_corners,
-    send_a, send_b, send_c, send_d, in_a, in_b, in_c, in_d,
-    forward, flipped, grad_wide, wide, total, padded, even, odd, slope, grad_even, grad_odd, grad_turned,
-    *rest,
+    grad_strips, grad_corners,
+    send_a, send_b, send_c, send_d, send_e, in_a, in_b, in_c, in_d, in_e,
+    forward, flipped, grad_wide, wide, total, padded, widened, even, odd, slope, grad_even, grad_odd,
+    turned_one, turned_two, masked, *rest,
 ):
-    sum_one, sum_two = rest[:9], rest[9:18]
     swap_sems, one_sems, two_sems = rest[18:]
     place = Place()
     me = place.me
@@ -723,8 +786,9 @@
     back_two = Swap(me, send_b, in_b, swap_sems.at[1])
     rims_two = Swap(me, send_c, in_c, swap_sems.at[2])
     back_one = Swap(me, send_d, in_d, swap_sems.at[3])
-    reduce_one = Sum(place, sum_one, one_sems)
-    reduce_two = Sum(place, sum_two, two_sems)
+    rims_grad = Swap(me, send_e, in_e, swap_sems.at[4])
+    reduce_one = Sum(place, rest[:9], one_sems)
+    reduce_two = Sum(place, rest[9:18], two_sems)
 
     for slot in range(2):
         for row in range(8):
@@ -734,6 +798,22 @@
     send_rims(table, strips, corners, send_a)
     pl.semaphore_wait(barrier, 29)
     rims_one.start()
+
+    grad_wide[...] = jnp.zeros_like(grad_wide)
+    for slot in range(2):
+        present = jnp.where(table[T_PRESENT + slot] > 0, 1.0, 0.0)
+        for row in range(8):
+            moved = blocks((product(turns[0], cotangent[slot, row]) * present).astype(BF16))
+            grad_blocks[slot, row] = moved
+            grad_wide[slot, 2 + row, 2:10] = moved
+    take_rims(grad_blocks, grad_strips, grad_corners)
+    for slot in range(2):
+        for side in range(4):
+            keep = jnp.where(piece_of(table, slot, 4 + side)[5] > 0, 1.0, 0.0).astype(BF16)
+            at = slot * 4 + side
+            grad_corners[at] = grad_corners[at] * keep
+    send_rims(table, grad_strips, grad_corners, send_e, T_GIVE_STRIP, T_GIVE_CORNER)
+    rims_grad.start()
 
     forward[...] = jnp.zeros_like(forward)
     flipped[...] = jnp.zeros_like(flipped)
@@ -747,13 +827,6 @@
                     forward[layer, at : at + 128, side * 128 : side * 128 + 128] = weight
                     at = (up * 4 + side + 2 - across) * 128
                     flipped[layer, at : at + 128, side * 128 : side * 128 + 128] = turned
-    grad_wide[...] = jnp.zeros_like(grad_wide)
-    for slot in range(2):
-        present = jnp.where(table[T_PRESENT + slot] > 0, 1.0, 0.0)
-        for row in range(8):
-            moved = blocks((product(turns[0], cotangent[slot, row]) * present).astype(BF16))
-            grad_blocks[slot, row] = moved
-            grad_wide[slot, 2 + row, 2:10] = moved
     for slot in range(2):
         for row in (0, 5):
             sources = [grad_wide[slot, row + 2 - up : row + 7 - up] for up in range(3)]
@@ -762,38 +835,83 @@
     give_back(table, wide, turns, send_b, given_strips, given_corners)
     back_two.start()
 
+    for slot in range(2):
+        for step in range(4):
+            at = slot * 1024 + step * 256
+            turned_two[:, at : at + 256] = cells(grad_blocks[slot, step * 2 : step * 2 + 2]).T
+    widened[...] = jnp.zeros_like(widened)
+    grad_even[...] = jnp.zeros_like(grad_even)
+    grad_odd[...] = jnp.zeros_like(grad_odd)
+    for slot in range(2):
+        padded[slot, 1:9, 1:9] = state_blocks[slot]
+
+    def arrange(rows_even, rows_odd, span):
+        def half_rows(slot, row):
+            return halves(padded[slot, row : row + 1, span])[0]
+
+        at = slice(span.start * 2, span.stop * 2)
+        for row in rows_even:
+            both = [half_rows(slot, row) for slot in range(2)]
+            even[row, at] = jnp.concatenate(both, axis=1).astype(BF16)
+        for row in rows_odd:
+            both = [shifted_up(half_rows(slot, row), half_rows(slot, row + 1)) for slot in range(2)]
+            odd[row, at] = jnp.concatenate(both, axis=1).astype(BF16)
+
+    arrange(range(1, 9), range(1, 8), slice(1, 9))
     rims_one.wait()
     widen(table, state_blocks, strips, corners, in_a, turns, padded)
-    for row in range(10):
-        both = [halves(padded[slot, row : row + 1])[0] for slot in range(2)]
-        even[row] = jnp.concatenate(both, axis=1).astype(BF16)
-    for row in range(9):
-        both = [
-            shifted_up(halves(padded[slot, row : row + 1])[0], halves(padded[slot, row + 1 : row + 2])[0])
-            for slot in range(2)
-        ]
-        odd[row] = jnp.concatenate(both, axis=1).astype(BF16)
+    arrange(range(1, 9), range(1, 8), slice(0, 1))
+    arrange(range(1, 9), range(1, 8), slice(9, 10))
+    arrange((), (0, 8), slice(0, 10))
     for row in (0, 4):
         sources = [odd[row : row + 4], even[row + 1 : row + 5], odd[row + 1 : row + 5]]
         result = paired_conv(sources, 1, 8, forward[0])
         hidden, slopes = gelu_parts(result)
         slope[row : row + 4] = slopes
         for slot in range(2):
-            part = hidden[:, :, slot * 8 : slot * 8 + 8].reshape(4, 8, 16, 128)
-            hidden_blocks[slot, row : row + 4] = part.astype(BF16)
+            part = hidden[:, :, slot * 8 : slot * 8 + 8].reshape(4, 8, 16, 128).astype(BF16)
+            hidden_blocks[slot, row : row + 4] = part
+            widened[slot, row + 1 : row + 5, 1:9] = part
     take_rims(hidden_blocks, strips, corners)
     send_rims(table, strips, corners, send_c)
     rims_two.start()
 
-    grad_even[...] = jnp.zeros_like(grad_even)
-    grad_odd[...] = jnp.zeros_like(grad_odd)
+    rims_grad.wait()
+    extra = rim_terms(table, in_e, grad_strips, grad_corners, strips, corners, turns, masked)
+    windows = []
+    for slot in range(2):
+        for row in (0, 4):
+            taps = [
+                cells(widened[slot, row + up : row + up + 4, across : across + 8])
+                for up in range(3)
+                for across in range(3)
+            ]
+            windows.append((slot * 1024 + row * 128, taps))
+    reduce_two.put(gradient_terms(turned_two, windows, extra))
+    broken = jnp.zeros((1, 16, 128), F32) + table[T_OVER].astype(F32)
+    for half in range(2):
+        reduce_one.half_send[half, 36:37] = jnp.zeros((1, 16, 128), BF16)
+        reduce_two.half_send[half, 36:37] = broken.astype(BF16)
+    reduce_two.one()
+
     back_two.wait()
     take_back(table, in_b, given_strips, given_corners, total)
     for row in range(8):
         both = [total[slot, row].astype(BF16).astype(F32).reshape(16, 8, 128) for slot in range(2)]
         grad = (jnp.concatenate(both, axis=1) * slope[row]).astype(BF16)
         grad_even[row + 1, 2:18] = grad
-        grad_turned[:, row * 256 : row * 256 + 256] = cells(grad).T
+        turned_one[:, row * 256 : row * 256 + 256] = cells(grad).T
+    reduce_two.two()
+    windows = []
+    for row in range(0, 8, 2):
+        taps = []
+        for source, at in ((odd, row), (even, row + 1), (odd, row + 1)):
+            for across in range(3):
+                taps.append(cells(source[at : at + 2, 1 + across : 17 + across]))
+        windows.append((row * 256, taps))
+    reduce_one.put(gradient_terms(turned_one, windows))
+    reduce_one.one()
+
     for row in range(9):
         low = grad_even[row, 2:18].astype(F32)
         high = grad_even[row + 1, 2:18].astype(F32)
@@ -802,72 +920,38 @@
             for slot in range(2)
         ]
         grad_odd[row + 1, 2:18] = jnp.concatenate(both, axis=1).astype(BF16)
-    for row in (0, 5):
+    reduce_one.two()
+
+    def returned(row):
         sources = [grad_odd[row + 1 : row + 6], grad_even[row : row + 5], grad_odd[row : row + 5]]
         result = paired_conv(sources, 0, 9, flipped[0])
         blank = jnp.zeros((5, 1, 8, 128), F32)
         for slot in range(2):
             part = jnp.concatenate([blank, result[:, :, slot * 8 : slot * 8 + 8], blank], axis=1)
             wide[slot, row : row + 5] = part.reshape(5, 10, 16, 128)
-    give_back(table, wide, turns, send_d, given_strips, given_corners)
-    back_one.start()
-    for slot in range(2):
-        total[slot] = wide[slot, 1:9, 1:9]
-
-    windows = []
-    for row in range(0, 8, 2):
-        taps = []
-        for source, at in ((odd, row), (even, row + 1), (odd, row + 1)):
-            for across in range(3):
-                taps.append(cells(source[at : at + 2, 1 + across : 17 + across]))
-        windows.append((row * 256, taps))
-    for tap, term in enumerate(gradient_terms(grad_turned, windows)):
-        reduce_one.put(tap * 8, blocks(term)[:4])
-        reduce_one.put(tap * 8 + 4, blocks(term)[4:])
-    blank = jnp.zeros((1, 16, 128), F32)
-    broken = blank + table[T_OVER].astype(F32)
-    for half in range(2):
-        reduce_one.half_send[half, 36:37] = blank.astype(BF16)
-        reduce_two.half_send[half, 36:37] = broken.astype(BF16)
-    reduce_one.one()
-
-    for slot in range(2):
-        for step in range(4):
-            at = slot * 1024 + step * 256
-            grad_turned[:, at : at + 256] = cells(grad_blocks[slot, step * 2 : step * 2 + 2]).T
-    rims_two.wait()
-    widen(table, hidden_blocks, strips, corners, in_c, turns, padded)
-    reduce_one.two()
-    windows = []
-    for slot in range(2):
-        for row in (0, 4):
-            taps = [
-                cells(padded[slot, row + up : row + up + 4, across : across + 8])
-                for up in range(3)
-                for across in range(3)
-            ]
-            windows.append((slot * 1024 + row * 128, taps))
-    for tap, term in enumerate(gradient_terms(grad_turned, windows)):
-        reduce_two.put(tap * 8, blocks(term)[:4])
-        reduce_two.put(tap * 8 + 4, blocks(term)[4:])
-    reduce_two.one()
-    reduce_one.three()
 
     def finish(slot):
         present = jnp.where(table[T_PRESENT + slot] > 0, 1.0, 0.0)
         for row in (0, 4):
-            sources = [padded[slot, row + up : row + up + 4] for up in range(3)]
+            sources = [widened[slot, row + up : row + up + 4] for up in range(3)]
             result = paired_conv(sources, 0, 4, forward[1])
             value = state_blocks[slot, row : row + 4].astype(F32) + result
             fresh[slot, row : row + 4] = (value * present).astype(BF16)
 
-    reduce_two.two()
+    returned(0)
+    returned(5)
+    give_back(table, wide, turns, send_d, given_strips, given_corners)
+    back_one.start()
+    for slot in range(2):
+        total[slot] = wide[slot, 1:9, 1:9]
+    reduce_two.three()
+    reduce_one.three()
+    rims_two.wait()
+    widen(table, hidden_blocks, strips, corners, in_c, turns, widened)
+    finish(0)
+    finish(1)
+    reduce_two.four()
     reduce_one.four()
-    finish(0)
-    reduce_two.three()
-    finish(1)
-    reduce_one.five()
-    reduce_two.four()
     back_one.wait()
     take_back(table, in_d, given_strips, given_corners, total)
     for slot in range(2):
@@ -875,8 +959,9 @@
         value = grad_blocks[slot].astype(F32) + total[slot]
         summed[slot] = (value * present).astype(BF16)
     reduce_two.five()
+    reduce_one.five()
+    reduce_two.end(sums, 1, over)
     reduce_one.end(sums, 0, None)
-    reduce_two.end(sums, 1, over)
 
 
 def settle(scale, fresh, summed, sums, back, next_state, cell_grad, kernel_grads):
@@ -956,19 +1041,21 @@
         scratch_shapes=[
             vmem(TILES, BF16), vmem(TILES, BF16), vmem(TILES, BF16),
             vmem(STRIPS, BF16), vmem(CORNERS, BF16), vmem(STRIPS, BF16), vmem(CORNERS, BF16),
+            vmem(STRIPS, BF16), vmem(CORNERS, BF16),
         ]
-        + [vmem(SENT, BF16)] * 8
+        + [vmem(SENT, BF16)] * 10
         + [
             vmem((2, 1536, 256), BF16), vmem((2, 1536, 256), BF16),
             vmem((2, 12, 12, 16, 128), BF16), vmem((2, 10, 10, 16, 128), F32), vmem(TILES, F32),
-            vmem((2, 10, 10, 16, 128), BF16), vmem((10, 20, 16, 128), BF16), vmem((9, 20, 16, 128), BF16),
+            vmem((2, 10, 10, 16, 128), BF16), vmem((2, 10, 10, 16, 128), BF16),
+            vmem((10, 20, 16, 128), BF16), vmem((9, 20, 16, 128), BF16),
             vmem((8, 16, 16, 128), F32), vmem((10, 20, 16, 128), BF16), vmem((11, 20, 16, 128), BF16),
-            vmem((128, 2048), BF16),
+            vmem((128, 2048), BF16), vmem((128, 2048), BF16), vmem((512, 1024), BF16),
         ]
         + sum_buffers()
         + sum_buffers()
         + [
-            pltpu.SemaphoreType.DMA((4, 2, 6)),
+            pltpu.SemaphoreType.DMA((5, 2, 6)),
             pltpu.SemaphoreType.DMA((2, 39)),
             pltpu.SemaphoreType.DMA((2, 39)),
         ],

time: 68.7 us -> 61.6 us (0.90)
  Pallas kernels: 65.4 us -> 58.4 us
    pallas_call x1, Pallas kernels: 58.3 us -> 51.2 us  [routed(): pl.pallas_call(whole, out_shape=[shape(TILES, BF16), shape(TILES, BF16),...]
where the time goes in v2:
time: 61.6 us; the launch traced here: 61.4 us
  Pallas kernels  58.4 us (95%)
  between operations  1.4 us (2%)
  local copies, waits for them, and re-layouts  1.37 us (2%)
    pallas_call x1, Pallas kernels, routed(): pl.pallas_call(whole, out_shape=[shape(TILES, BF16), shape(TILES, BF16),...  51.2 us
    pallas_call x1, Pallas kernels, routed(): pl.pallas_call(plan_kernel, out_shape=shape((T_SIZE,), jnp.int32), in_spe...  4.28 us
    pallas_call x1, Pallas kernels, finished(): pl.pallas_call(functools.partial(settle, scale), grid=(4,), out_shape=[sh...  2.87 us
    unnamed x20, local copies, waits for them, and re-layouts  1.37 us

profile of v2, /device:TPU:1, one launch (start us, length us, event | category | flops | bytes accessed | tf_op | source)
XLA Modules:
  0.0 61.4 jit_solution(10852227122275809653)
XLA Ops:
  0.6 0.0 copy-start.33
  0.6 0.0 copy-start.34
  0.7 0.0 copy-start.35
  0.7 0.0 copy-start
  0.7 0.0 copy-start.1
  0.7 0.0 copy-start.6
  0.7 0.0 copy-start.14
  0.7 4.3 %shard_map.119.table = s32[208]{0:T(256)} custom-call(s32[192]{0:T(256)} %slot_ref.1, s32[8,192]{1,0:T(8,128)} %bitcast.683, s32[8,192]{1,0:T(8,128)} %bitcast.684, s32[4,192]{1,0:T(4,128)} %bitcast.686), custom_call_target="tpu_custom_call" | custom-call | tf_op jit(solution)/shard_map/pallas_call | solution.py:1023
  5.0 51.2 %shard_map.120 = (bf16[2,8,8,16,128]{4,3,2,1,0:T(8,128)(2,1)}, bf16[2,8,8,16,128]{4,3,2,1,0:T(8,128)(2,1)}, bf16[2,72,16,128]{3,2,1,0:T(8,128)(2,1)}, s32[1]{0:T(128)}) custom-call(s32[208]{0:T(256)} %shard_map.119.table, bf16[2,8,128,128]{3,2,1,0:T(8,128)(2,1)} %bitcast.584, bf16[2,8,128,128]{3,2,1,0:T(8,128)(2,1)} %bitcast.626, ...), custom_call_target="tpu_custom_call" | custom-call | tf_op jit(solution)/shard_map/pallas_call | solution.py:1034
  56.9 0.0 copy-done.33
  56.9 0.0 copy-done.34
  56.9 0.0 copy-done.35
  56.9 0.0 copy-done
  56.9 0.0 copy-done.1
  56.9 0.0 copy-done.6
  56.9 0.0 copy-done.14
  56.9 3.2 %conditional.1 = (f32[2,3,3,128,128]{4,3,2,1,0:T(8,128)S(1)}, bf16[1,2,32,32,128]{4,3,2,1,0:T(8,128)(2,1)S(1)}, bf16[1,2,32,32,128]{4,3,2,1,0:T(8,128)(2,1)S(1)}) conditional(s32[]{:T(128)} %bitcast.240, (s32[192]{0:T(256)S(1)}, bf16[1,2,32,32,128]{4,3,2,1,0:T(8,128)(2,1)S(1)}, s32[192,4]{0,1:T(4,128)S(1)}, s32[192,8]{0,1:T(8,128)S(1)}, ...), branch_computations={%region_0.10_spmd, %region_7.11_spmd} | conditional | flops 3985077248 | bytes 308919744 | solution.py:1076
  57.2 2.9 %branch_1_fun.1 = (bf16[16,128,128]{2,1,0:T(8,128)(2,1)S(1)}, bf16[16,128,128]{2,1,0:T(8,128)(2,1)S(1)}, f32[144,16,128]{2,1,0:T(8,128)S(1)}) custom-call(bf16[16,8,16,128]{3,2,1,0:T(8,128)(2,1)} %bitcast.647, bf16[16,8,16,128]{3,2,1,0:T(8,128)(2,1)} %bitcast.648, bf16[144,16,128]{2,1,0:T(8,128)(2,1)} %bitcast.646, bf16[128,128]{1,0:T(8,128)(2,1)} %constant.169.clone.1.back), custom_call_target="tpu_custom_call" | custom-call | tf_op jit(solution)/shard_map/cond/branch_1_fun/pallas_call | solution.py:1005
  60.1 0.0 copy-start.11
  60.1 0.0 copy-start.18
  60.1 0.0 copy-start.19
  60.1 1.0 %copy-done.11 = f32[2,3,3,128,128]{4,3,2,1,0:T(8,128)} copy-done((f32[2,3,3,128,128]{4,3,2,1,0:T(8,128)}, f32[2,3,3,128,128]{4,3,2,1,0:T(8,128)S(1)}, u32[]{:S(2)}) %copy-start.11) | copy-done | bytes 1179672
  61.1 0.2 copy-done.18
  61.3 0.2 copy-done.19
Async XLA Ops:
  0.6 56.2 %copy-start.33 = (s32[192,8]{0,1:T(8,128)S(1)}, s32[192,8]{0,1:T(8,128)}, u32[]{:S(2)}) copy-start(s32[192,8]{0,1:T(8,128)} %param.21) | copy-start | bytes 18436
  0.6 56.2 %copy-start.34 = (s32[192,8]{0,1:T(8,128)S(1)}, s32[192,8]{0,1:T(8,128)}, u32[]{:S(2)}) copy-start(s32[192,8]{0,1:T(8,128)} %param.22) | copy-start | bytes 18436
  0.7 56.2 %copy-start.35 = (s32[192,4]{0,1:T(4,128)S(1)}, s32[192,4]{0,1:T(4,128)}, u32[]{:S(2)}) copy-start(s32[192,4]{0,1:T(4,128)} %param.23) | copy-start | bytes 9220
  0.7 56.2 %copy-start = (s32[192]{0:T(256)S(1)}, s32[192]{0:T(256)}, u32[]{:S(2)}) copy-start(s32[192]{0:T(256)} %slot_ref.1) | copy-start | bytes 2308
  0.7 56.2 %copy-start.1 = (bf16[1,2,32,32,128]{4,3,2,1,0:T(8,128)(2,1)S(1)}, bf16[1,2,32,32,128]{4,3,2,1,0:T(8,128)(2,1)}, u32[]{:S(2)}) copy-start(bf16[1,2,32,32,128]{4,3,2,1,0:T(8,128)(2,1)} %param.17) | copy-start | bytes 1572868
  0.7 56.2 %copy-start.6 = (bf16[1,2,32,32,128]{4,3,2,1,0:T(8,128)(2,1)S(1)}, bf16[1,2,32,32,128]{4,3,2,1,0:T(8,128)(2,1)}, u32[]{:S(2)}) copy-start(bf16[1,2,32,32,128]{4,3,2,1,0:T(8,128)(2,1)} %param.18) | copy-start | bytes 1572868
  0.7 56.2 %copy-start.14 = (bf16[2,3,3,128,128]{4,3,2,1,0:T(8,128)(2,1)S(1)}, bf16[2,3,3,128,128]{4,3,2,1,0:T(8,128)(2,1)}, u32[]{:S(2)}) copy-start(bf16[2,3,3,128,128]{4,3,2,1,0:T(8,128)(2,1)} %kernels.1) | copy-start | bytes 1769476
  60.1 1.0 %copy-start.11 = (f32[2,3,3,128,128]{4,3,2,1,0:T(8,128)}, f32[2,3,3,128,128]{4,3,2,1,0:T(8,128)S(1)}, u32[]{:S(2)}) copy-start(f32[2,3,3,128,128]{4,3,2,1,0:T(8,128)S(1)} %get-tuple-element.186) | copy-start | bytes 3538948
  60.1 1.2 %copy-start.18 = (bf16[1,2,32,32,128]{4,3,2,1,0:T(8,128)(2,1)}, bf16[1,2,32,32,128]{4,3,2,1,0:T(8,128)(2,1)S(1)}, u32[]{:S(2)}) copy-start(bf16[1,2,32,32,128]{4,3,2,1,0:T(8,128)(2,1)S(1)} %get-tuple-element.188) | copy-start | bytes 1572868
  60.1 1.3 %copy-start.19 = (bf16[1,2,32,32,128]{4,3,2,1,0:T(8,128)(2,1)}, bf16[1,2,32,32,128]{4,3,2,1,0:T(8,128)(2,1)S(1)}, u32[]{:S(2)}) copy-start(bf16[1,2,32,32,128]{4,3,2,1,0:T(8,128)(2,1)S(1)} %get-tuple-element.187) | copy-start | bytes 1572868

commit v3 on v2

--- a/solution.py
+++ b/solution.py
@@ -267,9 +267,10 @@
 
 MESH_ID = pl.DeviceIdType.MESH
 SPAN = 128
-STRIP_CAP = (1, 2, 2, 2, 2, 1)
-CORNER_CAP = 4
-PART = 20
+STRIP_SLOTS = (1, 2, 2, 2, 2, 1)
+CORNER_CAP = 3
+PART = CORNER_CAP + 16
+THIN = 9
 OFFSETS = (-3, -2, -1, 1, 2, 3)
 ORDER = (2, 3, 1, 4, 0, 5)
 SELF = 6
@@ -315,6 +316,35 @@
     return jnp.where(turn == 2, 1, once + thrice)
 
 
+def packings():
+    order = cell_order()
+    mats = permutations()
+    inner = (order[:2], order[:, 2:], order[2:], order[:, :2])
+    ends = (order[:2, 2:], order[2:, 2:], order[2:, :2], order[:2, :2])
+    pack = np.zeros((4, 64, 128), np.float32)
+    pack_corners = np.zeros((128, 128), np.float32)
+    for side in range(4):
+        for block in range(8):
+            for at, cell in enumerate(sorted(inner[side].reshape(-1))):
+                pack[side, block * 8 + at, block * 16 + cell] = 1
+        for at, cell in enumerate(sorted(ends[side].reshape(-1))):
+            for slot in range(2):
+                for copy in range(4):
+                    base = (slot * 4 + side) * 16
+                    pack_corners[base + copy * 4 + at, base + cell] = 1
+    unpack = np.zeros((16, 128, 64), np.float32)
+    unpack_corners = np.zeros((16, 16, 128), np.float32)
+    for turn in range(4):
+        for edge in range(4):
+            side = (edge + 2 + turn) % 4
+            flip = int(turn == 2 or (turn == 1 and side % 2 == 0) or (turn == 3 and side % 2 == 1))
+            unpack[turn * 4 + edge] = mats[2 + 2 * turn + flip] @ pack[side].T
+            four = pack_corners[side * 16 : side * 16 + 4, side * 16 : side * 16 + 16]
+            small = mats[2 + 2 * turn][:16, :16] @ four.T
+            unpack_corners[turn * 4 + edge] = np.tile(small, (1, 32))
+    return pack, pack_corners, unpack, unpack_corners
+
+
 def plan_kernel(slot_ref, near_ref, turn_ref, flag_ref, table, tile_at):
     me = lax.axis_index("space")
     for entry in range(T_SIZE):
@@ -353,7 +383,7 @@
                 hit = (tile >= 0) & (source // 2 == me)
                 turn = turn_ref[piece, row] & 3
                 entry = source % 2 * 4 + ((piece + 2 + turn) & 3)
-                cap = CORNER_CAP if kind else STRIP_CAP[where]
+                cap = CORNER_CAP if kind else (1, 2, 1 + core, 2 - core, 2, 1)[where]
                 rank = jnp.minimum(seen[kind], cap - 1)
                 if offset in (-3, 3):
                     over = over + jnp.where(hit & (core == (0 if offset < 0 else 1)), 1, 0)
@@ -380,7 +410,7 @@
                 match = jnp.where(offset == choice, valid, 0)
                 rank = rank + match * seen[kind][choice]
                 seen[kind][choice] = seen[kind][choice] + match
-            rank = jnp.minimum(rank, 3 if kind else 1)
+            rank = jnp.minimum(rank, CORNER_CAP - 1 if kind else 1)
             keep = valid
             if kind:
                 keep = valid * jnp.where(flag_ref[piece - 4, row] == 0, 1, 0)
@@ -433,10 +463,29 @@
 
 def send_rims(table, strips, corners, send, strip_list=T_STRIP_LIST, corner_list=T_CORNER_LIST):
     for where in range(6):
-        for rank in range(STRIP_CAP[where]):
-            send[where, 4 + rank * 8 : 12 + rank * 8] = strips[table[strip_list + where * 2 + rank]]
+        for rank in range(STRIP_SLOTS[where]):
+            at = CORNER_CAP + rank * 8
+            send[where, at : at + 8] = strips[table[strip_list + where * 2 + rank]]
         for rank in range(CORNER_CAP):
             send[where, rank] = corners[table[corner_list + where * 4 + rank]]
+
+
+def send_thin(table, strips, corners, send):
+    group = lax.broadcasted_iota(jnp.int32, (16, 128), 0) // 4
+    for where in range(6):
+        for rank in range(STRIP_SLOTS[where]):
+            send[where, 1 + rank * 4 : 5 + rank * 4] = strips[table[T_STRIP_LIST + where * 2 + rank]]
+        unit = corners[table[T_CORNER_LIST + where * 4]]
+        for rank in range(1, CORNER_CAP):
+            unit = jnp.where(group == rank, corners[table[T_CORNER_LIST + where * 4 + rank]], unit)
+        send[where, 0] = unit.astype(BF16)
+
+
+def thin_rims(strips, corners, pack, pack_corners, thin_strips, thin_corners):
+    for entry in range(8):
+        packed = product(pack[entry % 4], cells(strips[entry]))
+        thin_strips[entry] = blocks(packed.astype(BF16))
+    thin_corners[...] = blocks(product(pack_corners[...], cells(corners[...])))
 
 
 def corner_turns(table, turns, back):
@@ -457,7 +506,7 @@
         for edge in range(4):
             valid, where, rank, turn, entry, keep = piece_of(table, slot, edge)
             own = strips[entry]
-            other = arrived[jnp.minimum(where, 5), pl.ds(4 + rank * 8, 8)]
+            other = arrived[jnp.minimum(where, 5), pl.ds(CORNER_CAP + rank * 8, 8)]
             strip = jnp.where(where == SELF, own, other)
             strip = jnp.where(valid > 0, strip, jnp.zeros_like(strip))
             turned = product(turns[turn_matrix(turn, flips(edge, turn))], cells(strip))
@@ -488,6 +537,33 @@
     send_rims(table, strips, corners, send, T_GIVE_STRIP, T_GIVE_CORNER)
 
 
+def widen_thin(table, thin_strips, thin_corners, arrived, unpack, unpack_corners, padded):
+    for slot in range(2):
+        for edge in range(4):
+            valid, where, rank, turn, entry, keep = piece_of(table, slot, edge)
+            other = arrived[jnp.minimum(where, 5), pl.ds(1 + rank * 4, 4)]
+            strip = jnp.where(where == SELF, thin_strips[entry], other)
+            strip = jnp.where(valid > 0, strip, jnp.zeros_like(strip))
+            turned = product(unpack[turn * 4 + edge], cells(strip))
+            padded[(slot,) + BAND_OF[edge]] = blocks(turned.astype(BF16))
+    lane = lax.broadcasted_iota(jnp.int32, (16, 128), 1)
+    stack, parts = [], []
+    for slot in range(2):
+        for side in range(4):
+            valid, where, rank, turn, entry, keep = piece_of(table, slot, 4 + side)
+            block = jnp.where(where == SELF, thin_corners[entry], arrived[jnp.minimum(where, 5), 0].astype(F32))
+            stack.append(jnp.where(valid > 0, block, jnp.zeros_like(block)).astype(BF16))
+            first = (slot * 4 + side) * 16 + jnp.where(where == SELF, 0, rank) * 4
+            chosen = (lane >= first) & (lane < first + 4) & (keep > 0)
+            rows = unpack_corners[turn * 4 + side].astype(F32)
+            parts.append(jnp.where(chosen, rows, jnp.zeros_like(rows)).astype(BF16))
+    turned = product(jnp.concatenate(parts, axis=0), jnp.concatenate(stack, axis=0))
+    turned = blocks(turned.astype(BF16))
+    for slot in range(2):
+        for side in range(4):
+            padded[(slot,) + BLOCK_OF[side]] = turned[slot * 4 + side]
+
+
 def owner_of(table, kind, entry):
     code = table[T_ADD + kind * 16 + entry]
     turn = table[T_ADD + kind * 16 + 8 + entry]
@@ -497,7 +573,7 @@
 def copied_strip(code, arrived, strips):
     far = jnp.minimum(code, 11)
     near = jnp.clip(code - 12, 0, 7)
-    part = jnp.where(code < 12, arrived[far // 2, pl.ds(4 + far % 2 * 8, 8)], strips[near])
+    part = jnp.where(code < 12, arrived[far // 2, pl.ds(CORNER_CAP + far % 2 * 8, 8)], strips[near])
     return jnp.where(code == NOT_THERE, jnp.zeros_like(part), part)
 
 
@@ -595,20 +671,24 @@
 
 
 class Swap:
-    def __init__(self, me, send, arrived, sems):
+    def __init__(self, me, send, arrived, sems, corner_units=CORNER_CAP, strip_units=8):
         core = me % 2
-        far = 5 - 5 * core
+        far, mate, other = 5 - 5 * core, 3 - core, 2 + core
         self.copies = []
-        for where in (2, 3, 1, 4, far):
-            near = isinstance(where, int)
-            size = 4 + 8 * (STRIP_CAP[where] if near else STRIP_CAP[0])
-            offset = OFFSETS[where] if near else 3 - 6 * core
+        for where, offset, strips, send_at, recv_at in (
+            (other, 2 * core - 1, 1, 2, 2),
+            (1, -2, 2, 1, 4),
+            (4, 2, 2, 4, 1),
+            (far, 3 - 6 * core, 1, 0, 0),
+            (mate, 1 - 2 * core, 2, 3, 3),
+        ):
+            size = corner_units + strip_units * strips
             self.copies.append(
                 pltpu.make_async_remote_copy(
                     src_ref=send.at[where, pl.ds(0, size)],
                     dst_ref=arrived.at[5 - where, pl.ds(0, size)],
-                    send_sem=sems.at[0, where if near else 0],
-                    recv_sem=sems.at[1, 5 - where if near else 0],
+                    send_sem=sems.at[0, send_at],
+                    recv_sem=sems.at[1, recv_at],
                     device_id={"space": lax.rem(me + offset + SPAN, SPAN)},
                     device_id_type=MESH_ID,
                 )
@@ -759,14 +839,20 @@
 
 
 def whole(
-    table, state, cotangent, kernels, turns, fresh, summed, sums, over,
-    state_blocks, grad_blocks, hidden_blocks, strips, corners, given_strips, given_corners,
+    table, state_far, cotangent_far, kernels_far, turns_far, pack, pack_corners, unpack, unpack_corners,
+    fresh, summed, sums, over,
+    state, cotangent, kernels, turns, load_sems, thin_strips, thin_corners, state_blocks, grad_blocks, hidden_blocks, strips, corners, given_strips, given_corners,
     grad_strips, grad_corners,
     send_a, send_b, send_c, send_d, send_e, in_a, in_b, in_c, in_d, in_e,
     forward, flipped, grad_wide, wide, total, padded, widened, even, odd, slope, grad_even, grad_odd,
     turned_one, turned_two, masked, *rest,
 ):
     swap_sems, one_sems, two_sems = rest[18:]
+    loads = []
+    pairs = ((turns_far, turns), (state_far, state), (cotangent_far, cotangent), (kernels_far, kernels))
+    for index, (source, target) in enumerate(pairs):
+        loads.append(pltpu.make_async_copy(source, target, load_sems.at[index]))
+        loads[index].start()
     place = Place()
     me = place.me
     barrier = pltpu.get_barrier_semaphore()
@@ -782,7 +868,7 @@
     for step in range(1, 8):
         greet(place.at_line(lax.rem(place.z + step, 8)))
 
-    rims_one = Swap(me, send_a, in_a, swap_sems.at[0])
+    rims_one = Swap(me, send_a, in_a, swap_sems.at[0], 1, 4)
     back_two = Swap(me, send_b, in_b, swap_sems.at[1])
     rims_two = Swap(me, send_c, in_c, swap_sems.at[2])
     back_one = Swap(me, send_d, in_d, swap_sems.at[3])
@@ -790,16 +876,20 @@
     reduce_one = Sum(place, rest[:9], one_sems)
     reduce_two = Sum(place, rest[9:18], two_sems)
 
+    loads[0].wait()
+    loads[1].wait()
     for slot in range(2):
         for row in range(8):
             moved = product(turns[0], state[slot, row])
             state_blocks[slot, row] = blocks(moved.astype(BF16))
     take_rims(state_blocks, strips, corners)
-    send_rims(table, strips, corners, send_a)
+    thin_rims(strips, corners, pack, pack_corners, thin_strips, thin_corners)
+    send_thin(table, thin_strips, thin_corners, send_a)
     pl.semaphore_wait(barrier, 29)
     rims_one.start()
 
     grad_wide[...] = jnp.zeros_like(grad_wide)
+    loads[2].wait()
     for slot in range(2):
         present = jnp.where(table[T_PRESENT + slot] > 0, 1.0, 0.0)
         for row in range(8):
@@ -815,6 +905,7 @@
     send_rims(table, grad_strips, grad_corners, send_e, T_GIVE_STRIP, T_GIVE_CORNER)
     rims_grad.start()
 
+    loads[3].wait()
     forward[...] = jnp.zeros_like(forward)
     flipped[...] = jnp.zeros_like(flipped)
     for layer in range(2):
@@ -859,7 +950,7 @@
 
     arrange(range(1, 9), range(1, 8), slice(1, 9))
     rims_one.wait()
-    widen(table, state_blocks, strips, corners, in_a, turns, padded)
+    widen_thin(table, thin_strips, thin_corners, in_a, unpack, unpack_corners, padded)
     arrange(range(1, 9), range(1, 8), slice(0, 1))
     arrange(range(1, 9), range(1, 8), slice(9, 10))
     arrange((), (0, 8), slice(0, 10))
@@ -976,7 +1067,8 @@
 
 
 def specs(kinds):
-    return [pl.BlockSpec(memory_space=pltpu.SMEM if kind == "s" else pltpu.VMEM) for kind in kinds]
+    spaces = {"s": pltpu.SMEM, "v": pltpu.VMEM, "a": pl.ANY}
+    return [pl.BlockSpec(memory_space=spaces[kind]) for kind in kinds]
 
 
 def shape(dims, kind):
@@ -987,6 +1079,7 @@
 STRIPS = (8, 8, 16, 128)
 CORNERS = (8, 16, 128)
 SENT = (6, PART, 16, 128)
+THIN_SENT = (6, THIN, 16, 128)
 NATURAL = (2, 8, 128, 128)
 
 
@@ -1004,15 +1097,16 @@
 
     return pl.pallas_call(
         functools.partial(settle, scale),
-        grid=(4,),
+        grid=(2,),
         out_shape=[
             shape((16, 128, 128), BF16), shape((16, 128, 128), BF16), shape((2 * UNITS, 16, 128), F32)
         ],
         in_specs=[
-            rows(4, 8, 16, 128), rows(4, 8, 16, 128), rows(36, 16, 128),
+            rows(8, 8, 16, 128), rows(8, 8, 16, 128), rows(UNITS, 16, 128),
             pl.BlockSpec((128, 128), lambda step: (0, 0)),
         ],
-        out_specs=[rows(4, 128, 128), rows(4, 128, 128), rows(36, 16, 128)],
+        out_specs=[rows(8, 128, 128), rows(8, 128, 128), rows(UNITS, 16, 128)],
+        compiler_params=pltpu.CompilerParams(vmem_limit_bytes=10 * 1024 * 1024),
     )(
         fresh.reshape(16, 8, 16, 128), summed.reshape(16, 8, 16, 128),
         sums.reshape(2 * UNITS, 16, 128), back,
@@ -1036,14 +1130,19 @@
         out_shape=[
             shape(TILES, BF16), shape(TILES, BF16), shape((2, UNITS, 16, 128), BF16), shape((1,), jnp.int32)
         ],
-        in_specs=specs("svvvv"),
+        in_specs=specs("saaaavvvv"),
         out_specs=specs("vvvs"),
         scratch_shapes=[
+            vmem(NATURAL, BF16), vmem(NATURAL, BF16), vmem(kernels.shape, BF16), vmem(turns.shape, BF16),
+            pltpu.SemaphoreType.DMA((4,)), vmem((8, 4, 16, 128), BF16), vmem(CORNERS, F32),
             vmem(TILES, BF16), vmem(TILES, BF16), vmem(TILES, BF16),
             vmem(STRIPS, BF16), vmem(CORNERS, BF16), vmem(STRIPS, BF16), vmem(CORNERS, BF16),
             vmem(STRIPS, BF16), vmem(CORNERS, BF16),
         ]
-        + [vmem(SENT, BF16)] * 10
+        + [vmem(THIN_SENT, BF16)]
+        + [vmem(SENT, BF16)] * 4
+        + [vmem(THIN_SENT, BF16)]
+        + [vmem(SENT, BF16)] * 4
         + [
             vmem((2, 1536, 256), BF16), vmem((2, 1536, 256), BF16),
             vmem((2, 12, 12, 16, 128), BF16), vmem((2, 10, 10, 16, 128), F32), vmem(TILES, F32),
@@ -1064,7 +1163,7 @@
         ),
     )(
         table, cell_state.reshape(NATURAL), cotangent.reshape(NATURAL), kernels,
-        jnp.asarray(turns, BF16),
+        jnp.asarray(turns, BF16), *(jnp.asarray(part, BF16) for part in packings()),
     )
     back = jnp.asarray(turns[1], BF16)
     arrays = (cell_state, cotangent, kernels, slot_of_tile, neighbours, rotations, corner_flags)

time: 61.6 us -> 58.6 us (0.951)
  Pallas kernels: 58.4 us -> 54.4 us
  local copies, waits for them, and re-layouts: 1.37 us -> 2.12 us
    pallas_call x1, Pallas kernels: 51.2 us -> 48.3 us  [routed(): pl.pallas_call(whole, out_shape=[shape(TILES, BF16), shape(TILES, BF16),...]
    pallas_call x1, Pallas kernels: 2.87 us -> 1.83 us  [finished(): pl.pallas_call(functools.partial(settle, scale), grid=(2,), out_shape=[sh...]
    cond x0 -> x2, local copies, waits for them, and re-layouts: none -> 0.75 us
where the time goes in v3:
time: 58.6 us; the launch traced here: 58.3 us
  Pallas kernels  54.4 us (93%)
  local copies, waits for them, and re-layouts  2.12 us (4%)
  between operations  1.46 us (2%)
    pallas_call x1, Pallas kernels, routed(): pl.pallas_call(whole, out_shape=[shape(TILES, BF16), shape(TILES, BF16),...  48.3 us
    pallas_call x1, Pallas kernels, routed(): pl.pallas_call(plan_kernel, out_shape=shape((T_SIZE,), jnp.int32), in_spe...  4.3 us
    pallas_call x1, Pallas kernels, finished(): pl.pallas_call(functools.partial(settle, scale), grid=(2,), out_shape=[sh...  1.83 us
    unnamed x20, local copies, waits for them, and re-layouts  1.37 us

profile of v3, /device:TPU:1, one launch (start us, length us, event | category | flops | bytes accessed | tf_op | source)
XLA Modules:
  0.0 58.3 jit_solution(2687340831320533995)
XLA Ops:
  0.6 0.0 copy-start.34
  0.6 0.0 copy-start.35
  0.7 0.0 copy-start.36
  0.7 0.0 copy-start.1
  0.7 0.0 copy-start.2
  0.7 0.0 copy-start.7
  0.7 0.0 copy-start.15
  0.7 4.3 %shard_map.155.table = s32[208]{0:T(256)} custom-call(s32[192]{0:T(256)} %slot_ref.1, s32[8,192]{1,0:T(8,128)} %bitcast.683, s32[8,192]{1,0:T(8,128)} %bitcast.684, s32[4,192]{1,0:T(4,128)} %bitcast.686), custom_call_target="tpu_custom_call" | custom-call | tf_op jit(solution)/shard_map/pallas_call | solution.py:1117
  5.0 48.3 %shard_map.156 = (bf16[2,8,8,16,128]{4,3,2,1,0:T(8,128)(2,1)}, bf16[2,8,8,16,128]{4,3,2,1,0:T(8,128)(2,1)}, bf16[2,72,16,128]{3,2,1,0:T(8,128)(2,1)}, s32[1]{0:T(128)}) custom-call(s32[208]{0:T(256)} %shard_map.155.table, bf16[2,8,128,128]{3,2,1,0:T(8,128)(2,1)} %bitcast.584, bf16[2,8,128,128]{3,2,1,0:T(8,128)(2,1)} %bitcast.626, ...), custom_call_target="tpu_custom_call" | custom-call | tf_op jit(solution)/shard_map/pallas_call | solution.py:1128
  54.0 0.0 copy-done.34
  54.0 0.0 copy-done.35
  54.0 0.0 copy-done.36
  54.0 0.0 copy-done.1
  54.0 0.0 copy-done.2
  54.1 0.0 copy-done.7
  54.1 0.0 copy-done.15
  54.1 2.9 %conditional.1 = (f32[2,3,3,128,128]{4,3,2,1,0:T(8,128)S(1)}, bf16[1,2,32,32,128]{4,3,2,1,0:T(8,128)(2,1)S(1)}, bf16[1,2,32,32,128]{4,3,2,1,0:T(8,128)(2,1)S(1)}) conditional(s32[]{:T(128)} %bitcast.240, (s32[192]{0:T(256)S(1)}, bf16[1,2,32,32,128]{4,3,2,1,0:T(8,128)(2,1)S(1)}, s32[192,4]{0,1:T(4,128)S(1)}, s32[192,8]{0,1:T(8,128)S(1)}, ...), branch_computations={%region_0.10_spmd, %region_7.11_spmd} | conditional | flops 3985077248 | bytes 308919744 | solution.py:1175
  54.4 0.0 copy-start
  54.4 0.7 %copy-done = bf16[128,128]{1,0:T(8,128)(2,1)S(1)} copy-done((bf16[128,128]{1,0:T(8,128)(2,1)S(1)}, bf16[128,128]{1,0:T(8,128)(2,1)}, u32[]{:S(2)}) %copy-start) | copy-done | bytes 32792 | tf_op jit(solution)/shard_map/cond
  55.1 1.8 %branch_1_fun.1 = (bf16[16,128,128]{2,1,0:T(8,128)(2,1)S(1)}, bf16[16,128,128]{2,1,0:T(8,128)(2,1)S(1)}, f32[144,16,128]{2,1,0:T(8,128)S(1)}) custom-call(bf16[16,8,16,128]{3,2,1,0:T(8,128)(2,1)} %bitcast.647, bf16[16,8,16,128]{3,2,1,0:T(8,128)(2,1)} %bitcast.648, bf16[144,16,128]{2,1,0:T(8,128)(2,1)} %bitcast.646, bf16[128,128]{1,0:T(8,128)(2,1)S(1)} %copy-done), custom_call_target="tpu_custom_call" | custom-call | tf_op jit(solution)/shard_map/cond/branch_1_fun/pallas_call | solution.py:1098
  57.0 0.0 copy-start.12
  57.0 0.0 copy-start.19
  57.0 0.0 copy-start.20
  57.0 1.0 %copy-done.12 = f32[2,3,3,128,128]{4,3,2,1,0:T(8,128)} copy-done((f32[2,3,3,128,128]{4,3,2,1,0:T(8,128)}, f32[2,3,3,128,128]{4,3,2,1,0:T(8,128)S(1)}, u32[]{:S(2)}) %copy-start.12) | copy-done | bytes 1179672
  58.0 0.2 copy-done.19
  58.1 0.2 copy-done.20
Async XLA Ops:
  0.6 53.4 %copy-start.34 = (s32[192,8]{0,1:T(8,128)S(1)}, s32[192,8]{0,1:T(8,128)}, u32[]{:S(2)}) copy-start(s32[192,8]{0,1:T(8,128)} %param.25) | copy-start | bytes 18436
  0.6 53.4 %copy-start.35 = (s32[192,8]{0,1:T(8,128)S(1)}, s32[192,8]{0,1:T(8,128)}, u32[]{:S(2)}) copy-start(s32[192,8]{0,1:T(8,128)} %param.26) | copy-start | bytes 18436
  0.7 53.4 %copy-start.36 = (s32[192,4]{0,1:T(4,128)S(1)}, s32[192,4]{0,1:T(4,128)}, u32[]{:S(2)}) copy-start(s32[192,4]{0,1:T(4,128)} %param.27) | copy-start | bytes 9220
  0.7 53.4 %copy-start.1 = (s32[192]{0:T(256)S(1)}, s32[192]{0:T(256)}, u32[]{:S(2)}) copy-start(s32[192]{0:T(256)} %slot_ref.1) | copy-start | bytes 2308
  0.7 53.4 %copy-start.2 = (bf16[1,2,32,32,128]{4,3,2,1,0:T(8,128)(2,1)S(1)}, bf16[1,2,32,32,128]{4,3,2,1,0:T(8,128)(2,1)}, u32[]{:S(2)}) copy-start(bf16[1,2,32,32,128]{4,3,2,1,0:T(8,128)(2,1)} %param.21) | copy-start | bytes 1572868
  0.7 53.4 %copy-start.7 = (bf16[1,2,32,32,128]{4,3,2,1,0:T(8,128)(2,1)S(1)}, bf16[1,2,32,32,128]{4,3,2,1,0:T(8,128)(2,1)}, u32[]{:S(2)}) copy-start(bf16[1,2,32,32,128]{4,3,2,1,0:T(8,128)(2,1)} %param.22) | copy-start | bytes 1572868
  0.7 53.4 %copy-start.15 = (bf16[2,3,3,128,128]{4,3,2,1,0:T(8,128)(2,1)S(1)}, bf16[2,3,3,128,128]{4,3,2,1,0:T(8,128)(2,1)}, u32[]{:S(2)}) copy-start(bf16[2,3,3,128,128]{4,3,2,1,0:T(8,128)(2,1)} %kernels_far.1) | copy-start | bytes 1769476
  54.4 0.8 %copy-start = (bf16[128,128]{1,0:T(8,128)(2,1)S(1)}, bf16[128,128]{1,0:T(8,128)(2,1)}, u32[]{:S(2)}) copy-start(bf16[128,128]{1,0:T(8,128)(2,1)} %constant.181.clone.1.back) | copy-start | bytes 98308 | tf_op jit(solution)/shard_map/cond
  57.0 1.0 %copy-start.12 = (f32[2,3,3,128,128]{4,3,2,1,0:T(8,128)}, f32[2,3,3,128,128]{4,3,2,1,0:T(8,128)S(1)}, u32[]{:S(2)}) copy-start(f32[2,3,3,128,128]{4,3,2,1,0:T(8,128)S(1)} %get-tuple-element.186) | copy-start | bytes 3538948
  57.0 1.2 %copy-start.19 = (bf16[1,2,32,32,128]{4,3,2,1,0:T(8,128)(2,1)}, bf16[1,2,32,32,128]{4,3,2,1,0:T(8,128)(2,1)S(1)}, u32[]{:S(2)}) copy-start(bf16[1,2,32,32,128]{4,3,2,1,0:T(8,128)(2,1)S(1)} %get-tuple-element.188) | copy-start | bytes 1572868
  57.0 1.3 %copy-start.20 = (bf16[1,2,32,32,128]{4,3,2,1,0:T(8,128)(2,1)}, bf16[1,2,32,32,128]{4,3,2,1,0:T(8,128)(2,1)S(1)}, u32[]{:S(2)}) copy-start(bf16[1,2,32,32,128]{4,3,2,1,0:T(8,128)(2,1)S(1)} %get-tuple-element.187) | copy-start | bytes 1572868

commit v4 on v3

--- a/solution.py
+++ b/solution.py
@@ -332,72 +332,59 @@
                 for copy in range(4):
                     base = (slot * 4 + side) * 16
                     pack_corners[base + copy * 4 + at, base + cell] = 1
-    unpack = np.zeros((16, 128, 64), np.float32)
+    unpack = np.zeros((16, 128, 128), np.float32)
     unpack_corners = np.zeros((16, 16, 128), np.float32)
     for turn in range(4):
         for edge in range(4):
             side = (edge + 2 + turn) % 4
             flip = int(turn == 2 or (turn == 1 and side % 2 == 0) or (turn == 3 and side % 2 == 1))
-            unpack[turn * 4 + edge] = mats[2 + 2 * turn + flip] @ pack[side].T
+            unpack[turn * 4 + edge, :, :64] = mats[2 + 2 * turn + flip] @ pack[side].T
             four = pack_corners[side * 16 : side * 16 + 4, side * 16 : side * 16 + 16]
             small = mats[2 + 2 * turn][:16, :16] @ four.T
             unpack_corners[turn * 4 + edge] = np.tile(small, (1, 32))
     return pack, pack_corners, unpack, unpack_corners
 
 
-def plan_kernel(slot_ref, near_ref, turn_ref, flag_ref, table, tile_at):
-    me = lax.axis_index("space")
-    for entry in range(T_SIZE):
-        table[entry] = 0
-    for entry in range(8):
-        table[T_ADD + entry] = NOT_THERE
-        table[T_ADD + 16 + entry] = NOT_THERE
-    for rel in range(14):
-        tile_at[(me + rel // 2 - 3 + SPAN) % SPAN * 2 + rel % 2] = -1
-
-    def place(step, carry):
-        for inner in range(16):
-            tile = step * 16 + inner
-            tile_at[slot_ref[tile]] = tile
-        return carry
-
-    lax.fori_loop(0, slot_ref.shape[0] // 16, place, 0)
+def make_plan(me, order_ref, slot_ref, near_ref, turn_ref, flag_ref, table):
+    core = me % 2
+    order = order_ref[...]
+    spot = lax.broadcasted_iota(jnp.int32, order.shape, 1) + 1
     over = jnp.int32(0)
-    core = me % 2
-
-    def contribute(hit, kind, entry, code, turn):
-        place_at = jnp.where(hit, T_ADD + kind * 16 + entry, T_SPARE)
-        taken = jnp.where(hit & (table[place_at] != NOT_THERE), 1, 0)
-        table[place_at] = code
-        table[place_at + jnp.where(hit, 8, 0)] = jnp.where(hit, turn, code)
-        return taken
+    found = [[], []]
+
+    def tile_in(offset, slot):
+        number = jnp.max(jnp.where(order == (me + offset + SPAN) % SPAN * 2 + slot, spot, 0))
+        return number > 0, jnp.maximum(number - 1, 0)
 
     for where, offset in enumerate(OFFSETS):
+        lists = [[jnp.int32(0)] * 2, [jnp.int32(0)] * CORNER_CAP]
         seen = [jnp.int32(0), jnp.int32(0)]
         for slot in range(2):
-            tile = tile_at[(me + offset + SPAN) % SPAN * 2 + slot]
-            row = jnp.maximum(tile, 0)
+            there, row = tile_in(offset, slot)
             for piece in range(8):
                 kind = piece // 4
                 source = slot_ref[near_ref[piece, row]]
-                hit = (tile >= 0) & (source // 2 == me)
+                hit = there & (source // 2 == me)
                 turn = turn_ref[piece, row] & 3
-                entry = source % 2 * 4 + ((piece + 2 + turn) & 3)
+                packed = (source % 2 * 4 + ((piece + 2 + turn) & 3)) * 4 + turn + 1
                 cap = CORNER_CAP if kind else (1, 2, 1 + core, 2 - core, 2, 1)[where]
-                rank = jnp.minimum(seen[kind], cap - 1)
+                late = seen[kind] >= cap
                 if offset in (-3, 3):
-                    over = over + jnp.where(hit & (core == (0 if offset < 0 else 1)), 1, 0)
-                over = over + jnp.where(hit & (seen[kind] >= cap), 1, 0)
+                    late = late | (core == (0 if offset < 0 else 1))
+                over = over + jnp.where(hit & late, 1, 0)
+                for rank, old in enumerate(lists[kind]):
+                    lists[kind][rank] = jnp.where(hit & (seen[kind] == rank), packed, old)
                 seen[kind] = seen[kind] + jnp.where(hit, 1, 0)
-                width = 4 if kind else 2
-                place_at = (T_CORNER_LIST if kind else T_STRIP_LIST) + where * width + rank
-                table[jnp.where(hit, place_at, T_SPARE)] = entry
-                over = over + contribute(hit, kind, entry, where * width + rank, turn)
+        for kind, base in enumerate((T_STRIP_LIST, T_CORNER_LIST)):
+            for rank, packed in enumerate(lists[kind]):
+                code = where * (4 if kind else 2) + rank
+                table[base + code] = jnp.maximum(packed - 1, 0) // 4
+                found[kind].append((packed, code))
     seen = [[jnp.int32(0)] * 7, [jnp.int32(0)] * 7]
-    for slot in range(2):
-        tile = tile_at[me * 2 + slot]
-        row = jnp.maximum(tile, 0)
-        valid = jnp.where(tile >= 0, 1, 0)
+    given = [[], []]
+    for slot in range(2):
+        there, row = tile_in(0, slot)
+        valid = jnp.where(there, 1, 0)
         table[T_PRESENT + slot] = valid
         for piece in range(8):
             kind = piece // 4
@@ -416,18 +403,31 @@
                 keep = valid * jnp.where(flag_ref[piece - 4, row] == 0, 1, 0)
             entry = source % 2 * 4 + ((piece + 2 + turn) & 3)
             base = T_PIECES + (slot * 8 + piece) * 6
-            table[base] = valid
-            table[base + 1] = where
-            table[base + 2] = rank
-            table[base + 3] = turn
-            table[base + 4] = entry
-            table[base + 5] = keep
+            for field, value in enumerate((valid, where, rank, turn, entry, keep)):
+                table[base + field] = value
             mine = slot * 4 + piece % 4
-            own = (valid > 0) & (where == SELF)
-            away = (valid > 0) & (where != SELF)
-            place_at = (T_GIVE_CORNER if kind else T_GIVE_STRIP) + where * (4 if kind else 2) + rank
-            table[jnp.where(away, place_at, T_SPARE)] = mine
-            over = over + contribute(own, kind, entry, (24 if kind else 12) + mine, turn)
+            own = there & (where == SELF)
+            found[kind].append((jnp.where(own, entry * 4 + turn + 1, 0), (24 if kind else 12) + mine))
+            code = where * (4 if kind else 2) + rank
+            given[kind].append((jnp.where(there & (where != SELF), code, -1), mine))
+    for kind, base in enumerate((T_GIVE_STRIP, T_GIVE_CORNER)):
+        for where in range(6):
+            for rank in range(CORNER_CAP if kind else 2):
+                code = where * (4 if kind else 2) + rank
+                chosen = jnp.int32(0)
+                for place, mine in given[kind]:
+                    chosen = jnp.where(place == code, mine, chosen)
+                table[base + code] = chosen
+        for entry in range(8):
+            chosen, count = jnp.int32(NOT_THERE * 4), jnp.int32(0)
+            for packed, code in found[kind]:
+                turn = packed - 1 - entry * 4
+                hit = (turn >= 0) & (turn < 4)
+                chosen = jnp.where(hit, code * 4 + turn, chosen)
+                count = count + jnp.where(hit, 1, 0)
+            table[T_ADD + kind * 16 + entry] = chosen // 4
+            table[T_ADD + kind * 16 + 8 + entry] = chosen & 3
+            over = over + jnp.maximum(count - 1, 0)
     table[T_OVER] = over
 
 
@@ -544,7 +544,7 @@
             other = arrived[jnp.minimum(where, 5), pl.ds(1 + rank * 4, 4)]
             strip = jnp.where(where == SELF, thin_strips[entry], other)
             strip = jnp.where(valid > 0, strip, jnp.zeros_like(strip))
-            turned = product(unpack[turn * 4 + edge], cells(strip))
+            turned = product(unpack[turn * 4 + edge][:, :64], cells(strip))
             padded[(slot,) + BAND_OF[edge]] = blocks(turned.astype(BF16))
     lane = lax.broadcasted_iota(jnp.int32, (16, 128), 1)
     stack, parts = [], []
@@ -839,9 +839,10 @@
 
 
 def whole(
-    table, state_far, cotangent_far, kernels_far, turns_far, pack, pack_corners, unpack, unpack_corners,
+    slot_ref, near_ref, turn_ref, flag_ref, order_ref,
+    state_far, cotangent_far, kernels_far, turns_far, unpack_far, pack, pack_corners, unpack_corners,
     fresh, summed, sums, over,
-    state, cotangent, kernels, turns, load_sems, thin_strips, thin_corners, state_blocks, grad_blocks, hidden_blocks, strips, corners, given_strips, given_corners,
+    table, state, cotangent, kernels, turns, unpack, load_sems, thin_strips, thin_corners, state_blocks, grad_blocks, hidden_blocks, strips, corners, given_strips, given_corners,
     grad_strips, grad_corners,
     send_a, send_b, send_c, send_d, send_e, in_a, in_b, in_c, in_d, in_e,
     forward, flipped, grad_wide, wide, total, padded, widened, even, odd, slope, grad_even, grad_odd,
@@ -849,7 +850,10 @@
 ):
     swap_sems, one_sems, two_sems = rest[18:]
     loads = []
-    pairs = ((turns_far, turns), (state_far, state), (cotangent_far, cotangent), (kernels_far, kernels))
+    pairs = (
+        (turns_far, turns), (state_far, state), (cotangent_far, cotangent), (kernels_far, kernels),
+        (unpack_far, unpack),
+    )
     for index, (source, target) in enumerate(pairs):
         loads.append(pltpu.make_async_copy(source, target, load_sems.at[index]))
         loads[index].start()
@@ -876,6 +880,7 @@
     reduce_one = Sum(place, rest[:9], one_sems)
     reduce_two = Sum(place, rest[9:18], two_sems)
 
+    make_plan(me, order_ref, slot_ref, near_ref, turn_ref, flag_ref, table)
     loads[0].wait()
     loads[1].wait()
     for slot in range(2):
@@ -949,6 +954,7 @@
             odd[row, at] = jnp.concatenate(both, axis=1).astype(BF16)
 
     arrange(range(1, 9), range(1, 8), slice(1, 9))
+    loads[4].wait()
     rims_one.wait()
     widen_thin(table, thin_strips, thin_corners, in_a, unpack, unpack_corners, padded)
     arrange(range(1, 9), range(1, 8), slice(0, 1))
@@ -1114,27 +1120,22 @@
 
 
 def routed(cell_state, cotangent, kernels, slot_of_tile, neighbours, rotations, corner_flags):
-    table = pl.pallas_call(
-        plan_kernel,
-        out_shape=shape((T_SIZE,), jnp.int32),
-        in_specs=specs("ssss"),
-        out_specs=specs("s")[0],
-        scratch_shapes=[pltpu.SMEM((2 * SPAN,), jnp.int32)],
-    )(slot_of_tile, neighbours.T, rotations.T, corner_flags.T)
     scale = 1.0 / math.sqrt(
         cell_state.shape[0] * lax.axis_size("dp") * slot_of_tile.shape[0] * cell_state.shape[2] ** 2
     )
     turns = permutations()
+    pack, pack_corners, unpack, unpack_corners = packings()
     fresh, summed, sums, over = pl.pallas_call(
         whole,
         out_shape=[
             shape(TILES, BF16), shape(TILES, BF16), shape((2, UNITS, 16, 128), BF16), shape((1,), jnp.int32)
         ],
-        in_specs=specs("saaaavvvv"),
+        in_specs=specs("ssssvaaaaavvv"),
         out_specs=specs("vvvs"),
         scratch_shapes=[
+            pltpu.SMEM((T_SIZE,), jnp.int32),
             vmem(NATURAL, BF16), vmem(NATURAL, BF16), vmem(kernels.shape, BF16), vmem(turns.shape, BF16),
-            pltpu.SemaphoreType.DMA((4,)), vmem((8, 4, 16, 128), BF16), vmem(CORNERS, F32),
+            vmem((16, 128, 128), BF16), pltpu.SemaphoreType.DMA((5,)), vmem((8, 4, 16, 128), BF16), vmem(CORNERS, F32),
             vmem(TILES, BF16), vmem(TILES, BF16), vmem(TILES, BF16),
             vmem(STRIPS, BF16), vmem(CORNERS, BF16), vmem(STRIPS, BF16), vmem(CORNERS, BF16),
             vmem(STRIPS, BF16), vmem(CORNERS, BF16),
@@ -1162,8 +1163,9 @@
             vmem_limit_bytes=VMEM_BYTES, collective_id=1, has_side_effects=True
         ),
     )(
-        table, cell_state.reshape(NATURAL), cotangent.reshape(NATURAL), kernels,
-        jnp.asarray(turns, BF16), *(jnp.asarray(part, BF16) for part in packings()),
+        slot_of_tile, neighbours.T, rotations.T, corner_flags.T, slot_of_tile.reshape(1, -1),
+        cell_state.reshape(NATURAL), cotangent.reshape(NATURAL), kernels, jnp.asarray(turns, BF16),
+        *(jnp.asarray(part, BF16) for part in (unpack, pack, pack_corners, unpack_corners)),
     )
     back = jnp.asarray(turns[1], BF16)
     arrays = (cell_state, cotangent, kernels, slot_of_tile, neighbours, rotations, corner_flags)

time: 58.6 us -> 53.3 us (0.910)
  Pallas kernels: 54.4 us -> 49.3 us
    pallas_call x1 -> x0, Pallas kernels: 4.3 us -> none  [routed(): pl.pallas_call(plan_kernel, out_shape=shape((T_SIZE,), jnp.int32), in_spe...]
    pallas_call x1, Pallas kernels: 48.3 us -> 47.5 us  [routed(): pl.pallas_call(whole, out_shape=[shape(TILES, BF16), shape(TILES, BF16),...]
where the time goes in v4:
time: 53.3 us; the launch traced here: 53.1 us
  Pallas kernels  49.3 us (92%)
  local copies, waits for them, and re-layouts  2.11 us (4%)
  between operations  1.46 us (3%)
    pallas_call x1, Pallas kernels, routed(): pl.pallas_call(whole, out_shape=[shape(TILES, BF16), shape(TILES, BF16),...  47.5 us
    pallas_call x1, Pallas kernels, finished(): pl.pallas_call(functools.partial(settle, scale), grid=(2,), out_shape=[sh...  1.83 us
    unnamed x20, local copies, waits for them, and re-layouts  1.36 us

profile of v4, /device:TPU:1, one launch (start us, length us, event | category | flops | bytes accessed | tf_op | source)
XLA Modules:
  0.0 53.1 jit_solution(12094361527066920151)
XLA Ops:
  0.6 0.0 copy-start.34
  0.6 0.0 copy-start.35
  0.7 0.0 copy-start.36
  0.7 0.0 copy-start.1
  0.7 0.0 copy-start.2
  0.7 0.0 copy-start.7
  0.7 0.0 copy-start.15
  0.7 47.5 %shard_map.155 = (bf16[2,8,8,16,128]{4,3,2,1,0:T(8,128)(2,1)}, bf16[2,8,8,16,128]{4,3,2,1,0:T(8,128)(2,1)}, bf16[2,72,16,128]{3,2,1,0:T(8,128)(2,1)}, s32[1]{0:T(128)}) custom-call(s32[192]{0:T(256)} %slot_ref.1, s32[8,192]{1,0:T(8,128)} %bitcast.685, s32[8,192]{1,0:T(8,128)} %bitcast.686, s32[4,192]{1,0:T(4,128)} %bitcast.687, s32[1,192]{1,0:T(1,128)} %bitcast.585, ...), custom_call_target="tpu_custom_call" | custom-call | tf_op jit(solution)/shard_map/pallas_call | solution.py:1128
  48.8 0.0 copy-done.34
  48.8 0.0 copy-done.35
  48.9 0.0 copy-done.36
  48.9 0.0 copy-done.1
  48.9 0.0 copy-done.2
  48.9 0.0 copy-done.7
  48.9 0.0 copy-done.15
  48.9 2.9 %conditional.1 = (f32[2,3,3,128,128]{4,3,2,1,0:T(8,128)S(1)}, bf16[1,2,32,32,128]{4,3,2,1,0:T(8,128)(2,1)S(1)}, bf16[1,2,32,32,128]{4,3,2,1,0:T(8,128)(2,1)S(1)}) conditional(s32[]{:T(128)} %bitcast.241, (s32[192]{0:T(256)S(1)}, bf16[1,2,32,32,128]{4,3,2,1,0:T(8,128)(2,1)S(1)}, s32[192,4]{0,1:T(4,128)S(1)}, s32[192,8]{0,1:T(8,128)S(1)}, ...), branch_computations={%region_0.10_spmd, %region_7.11_spmd} | conditional | flops 3985077248 | bytes 308919744 | solution.py:1177
  49.2 0.0 copy-start
  49.2 0.7 %copy-done = bf16[128,128]{1,0:T(8,128)(2,1)S(1)} copy-done((bf16[128,128]{1,0:T(8,128)(2,1)S(1)}, bf16[128,128]{1,0:T(8,128)(2,1)}, u32[]{:S(2)}) %copy-start) | copy-done | bytes 32792 | tf_op jit(solution)/shard_map/cond
  49.9 1.8 %branch_1_fun.1 = (bf16[16,128,128]{2,1,0:T(8,128)(2,1)S(1)}, bf16[16,128,128]{2,1,0:T(8,128)(2,1)S(1)}, f32[144,16,128]{2,1,0:T(8,128)S(1)}) custom-call(bf16[16,8,16,128]{3,2,1,0:T(8,128)(2,1)} %bitcast.649, bf16[16,8,16,128]{3,2,1,0:T(8,128)(2,1)} %bitcast.650, bf16[144,16,128]{2,1,0:T(8,128)(2,1)} %bitcast.648, bf16[128,128]{1,0:T(8,128)(2,1)S(1)} %copy-done), custom_call_target="tpu_custom_call" | custom-call | tf_op jit(solution)/shard_map/cond/branch_1_fun/pallas_call | solution.py:1104
  51.8 0.0 copy-start.12
  51.8 0.0 copy-start.19
  51.8 0.0 copy-start.20
  51.8 1.0 %copy-done.12 = f32[2,3,3,128,128]{4,3,2,1,0:T(8,128)} copy-done((f32[2,3,3,128,128]{4,3,2,1,0:T(8,128)}, f32[2,3,3,128,128]{4,3,2,1,0:T(8,128)S(1)}, u32[]{:S(2)}) %copy-start.12) | copy-done | bytes 1179672
  52.8 0.2 copy-done.19
  53.0 0.2 copy-done.20
Async XLA Ops:
  0.6 48.2 %copy-start.34 = (s32[192,8]{0,1:T(8,128)S(1)}, s32[192,8]{0,1:T(8,128)}, u32[]{:S(2)}) copy-start(s32[192,8]{0,1:T(8,128)} %param.25) | copy-start | bytes 18436
  0.6 48.2 %copy-start.35 = (s32[192,8]{0,1:T(8,128)S(1)}, s32[192,8]{0,1:T(8,128)}, u32[]{:S(2)}) copy-start(s32[192,8]{0,1:T(8,128)} %param.26) | copy-start | bytes 18436
  0.7 48.2 %copy-start.36 = (s32[192,4]{0,1:T(4,128)S(1)}, s32[192,4]{0,1:T(4,128)}, u32[]{:S(2)}) copy-start(s32[192,4]{0,1:T(4,128)} %param.27) | copy-start | bytes 9220
  0.7 48.2 %copy-start.1 = (s32[192]{0:T(256)S(1)}, s32[192]{0:T(256)}, u32[]{:S(2)}) copy-start(s32[192]{0:T(256)} %slot_ref.1) | copy-start | bytes 2308
  0.7 48.2 %copy-start.2 = (bf16[1,2,32,32,128]{4,3,2,1,0:T(8,128)(2,1)S(1)}, bf16[1,2,32,32,128]{4,3,2,1,0:T(8,128)(2,1)}, u32[]{:S(2)}) copy-start(bf16[1,2,32,32,128]{4,3,2,1,0:T(8,128)(2,1)} %param.21) | copy-start | bytes 1572868
  0.7 48.2 %copy-start.7 = (bf16[1,2,32,32,128]{4,3,2,1,0:T(8,128)(2,1)S(1)}, bf16[1,2,32,32,128]{4,3,2,1,0:T(8,128)(2,1)}, u32[]{:S(2)}) copy-start(bf16[1,2,32,32,128]{4,3,2,1,0:T(8,128)(2,1)} %param.22) | copy-start | bytes 1572868
  0.7 48.2 %copy-start.15 = (bf16[2,3,3,128,128]{4,3,2,1,0:T(8,128)(2,1)S(1)}, bf16[2,3,3,128,128]{4,3,2,1,0:T(8,128)(2,1)}, u32[]{:S(2)}) copy-start(bf16[2,3,3,128,128]{4,3,2,1,0:T(8,128)(2,1)} %kernels_far.1) | copy-start | bytes 1769476
  49.2 0.8 %copy-start = (bf16[128,128]{1,0:T(8,128)(2,1)S(1)}, bf16[128,128]{1,0:T(8,128)(2,1)}, u32[]{:S(2)}) copy-start(bf16[128,128]{1,0:T(8,128)(2,1)} %constant.181.clone.1.back) | copy-start | bytes 98308 | tf_op jit(solution)/shard_map/cond
  51.8 1.0 %copy-start.12 = (f32[2,3,3,128,128]{4,3,2,1,0:T(8,128)}, f32[2,3,3,128,128]{4,3,2,1,0:T(8,128)S(1)}, u32[]{:S(2)}) copy-start(f32[2,3,3,128,128]{4,3,2,1,0:T(8,128)S(1)} %get-tuple-element.186) | copy-start | bytes 3538948
  51.8 1.2 %copy-start.19 = (bf16[1,2,32,32,128]{4,3,2,1,0:T(8,128)(2,1)}, bf16[1,2,32,32,128]{4,3,2,1,0:T(8,128)(2,1)S(1)}, u32[]{:S(2)}) copy-start(bf16[1,2,32,32,128]{4,3,2,1,0:T(8,128)(2,1)S(1)} %get-tuple-element.188) | copy-start | bytes 1572868
  51.8 1.3 %copy-start.20 = (bf16[1,2,32,32,128]{4,3,2,1,0:T(8,128)(2,1)}, bf16[1,2,32,32,128]{4,3,2,1,0:T(8,128)(2,1)S(1)}, u32[]{:S(2)}) copy-start(bf16[1,2,32,32,128]{4,3,2,1,0:T(8,128)(2,1)S(1)} %get-tuple-element.187) | copy-start | bytes 1572868

commit v5 on v4

--- a/solution.py
+++ b/solution.py
@@ -345,7 +345,7 @@
     return pack, pack_corners, unpack, unpack_corners
 
 
-def make_plan(me, order_ref, slot_ref, near_ref, turn_ref, flag_ref, table):
+def plan_sends(me, order_ref, slot_ref, near_ref, turn_ref, table):
     core = me % 2
     order = order_ref[...]
     spot = lax.broadcasted_iota(jnp.int32, order.shape, 1) + 1
@@ -380,6 +380,10 @@
                 code = where * (4 if kind else 2) + rank
                 table[base + code] = jnp.maximum(packed - 1, 0) // 4
                 found[kind].append((packed, code))
+    return tile_in, found, over
+
+
+def plan_pieces(me, tile_in, found, slot_ref, near_ref, turn_ref, flag_ref, table):
     seen = [[jnp.int32(0)] * 7, [jnp.int32(0)] * 7]
     given = [[], []]
     for slot in range(2):
@@ -418,6 +422,10 @@
                 for place, mine in given[kind]:
                     chosen = jnp.where(place == code, mine, chosen)
                 table[base + code] = chosen
+
+
+def plan_sums(found, over, table):
+    for kind in range(2):
         for entry in range(8):
             chosen, count = jnp.int32(NOT_THERE * 4), jnp.int32(0)
             for packed, code in found[kind]:
@@ -606,29 +614,55 @@
 CORNER_TAPS = ((0, 2), (2, 2), (2, 0), (0, 0))
 
 
-def rim_terms(table, arrived, given_strips, given_corners, strips, corners, turns, masked):
+def rim_terms(
+    table, arrived, grad_strips, grad_corners, strips, corners, turns, edge_weights, corner_weights, masked, total
+):
     rims = []
+    blank = jnp.zeros((16, 128), BF16)
+
+    def shifts(value, order):
+        longer = jnp.concatenate([blank, value, blank], axis=0)
+        return jnp.concatenate([longer[step * 16 : step * 16 + 128] for step in order], axis=1)
+
     for entry in range(8):
         code, turn, edge = owner_of(table, 0, entry)
-        grad = cells(copied_strip(code, arrived, given_strips)).T
+        strip = cells(copied_strip(code, arrived, grad_strips))
+        grad = strip.T
         for choice in range(4):
             chosen = jnp.where(edge == choice, grad, jnp.zeros_like(grad))
             masked[choice * 128 : choice * 128 + 128, entry * 128 : entry * 128 + 128] = chosen
-        band = product(turns[turn_matrix(turn, flips(edge, turn))], cells(strips[entry])).astype(BF16)
-        blank = jnp.zeros((16, 128), BF16)
-        longer = jnp.concatenate([blank, band, blank], axis=0)
-        rims.append(jnp.concatenate([longer[step * 16 : step * 16 + 128] for step in range(3)], axis=1))
+        flip = flips(edge, turn)
+        band = product(turns[turn_matrix(turn, flip)], cells(strips[entry])).astype(BF16)
+        rims.append(shifts(band, (0, 1, 2)))
+        ring = product(shifts(strip, (2, 1, 0)), edge_weights[edge]).astype(BF16)
+        at = (entry // 4,) + EDGE_OF[entry % 4]
+        total[at] = total[at] + blocks(product(turns[turn_matrix((4 - turn) & 3, flip)], ring))
     edges = product(masked[...], jnp.concatenate(rims, axis=0))
     lane = lax.broadcasted_iota(jnp.int32, (128, 128), 1) // 16
     which = jnp.zeros((128, 128), jnp.int32)
-    grads, parts = [], []
+    grads, parts, backs, sides = [], [], [], []
     for entry in range(8):
         code, turn, side = owner_of(table, 1, entry)
-        grads.append(copied_corner(code, arrived, given_corners))
+        grads.append(copied_corner(code, arrived, grad_corners))
+        sides.append(side)
+        backs.append(turns[turn_matrix((4 - turn) & 3, 0)][entry * 16 : entry * 16 + 16])
         which = jnp.where(lane == entry, side, which)
         parts.append(turns[turn_matrix(turn, 0)][entry * 16 : entry * 16 + 16])
     block = product(jnp.concatenate(parts, axis=0), cells(corners[...])).astype(BF16)
-    grad = jnp.concatenate(grads, axis=0).astype(F32).T
+    stack = jnp.concatenate(grads, axis=0)
+    rings = product(stack, corner_weights[...])
+    chosen = []
+    for entry in range(8):
+        rows = rings[entry * 16 : entry * 16 + 16]
+        value = rows[:, :128]
+        for choice in range(1, 4):
+            value = jnp.where(sides[entry] == choice, rows[:, choice * 128 : choice * 128 + 128], value)
+        chosen.append(value.astype(BF16))
+    rings = blocks(product(jnp.concatenate(backs, axis=0), jnp.concatenate(chosen, axis=0)))
+    for entry in range(8):
+        at = (entry // 4,) + CORNER_OF[entry % 4]
+        total[at] = total[at] + rings[entry]
+    grad = stack.astype(F32).T
     spread = [jnp.where(which == choice, grad, jnp.zeros_like(grad)) for choice in range(4)]
     ends = product(jnp.concatenate(spread, axis=0).astype(BF16), block)
     sums = [None] * 9
@@ -841,10 +875,10 @@
 def whole(
     slot_ref, near_ref, turn_ref, flag_ref, order_ref,
     state_far, cotangent_far, kernels_far, turns_far, unpack_far, pack, pack_corners, unpack_corners,
-    fresh, summed, sums, over,
-    table, state, cotangent, kernels, turns, unpack, load_sems, thin_strips, thin_corners, state_blocks, grad_blocks, hidden_blocks, strips, corners, given_strips, given_corners,
+    fresh_far, summed_far, sums, over,
+    fresh, summed, edge_weights, corner_weights, table, state, cotangent, kernels, turns, unpack, load_sems, thin_strips, thin_corners, state_blocks, grad_blocks, hidden_blocks, strips, corners, given_strips, given_corners,
     grad_strips, grad_corners,
-    send_a, send_b, send_c, send_d, send_e, in_a, in_b, in_c, in_d, in_e,
+    send_a, send_c, send_d, send_e, in_a, in_c, in_d, in_e,
     forward, flipped, grad_wide, wide, total, padded, widened, even, odd, slope, grad_even, grad_odd,
     turned_one, turned_two, masked, *rest,
 ):
@@ -873,14 +907,13 @@
         greet(place.at_line(lax.rem(place.z + step, 8)))
 
     rims_one = Swap(me, send_a, in_a, swap_sems.at[0], 1, 4)
-    back_two = Swap(me, send_b, in_b, swap_sems.at[1])
-    rims_two = Swap(me, send_c, in_c, swap_sems.at[2])
-    back_one = Swap(me, send_d, in_d, swap_sems.at[3])
-    rims_grad = Swap(me, send_e, in_e, swap_sems.at[4])
+    rims_two = Swap(me, send_c, in_c, swap_sems.at[1])
+    back_one = Swap(me, send_d, in_d, swap_sems.at[2])
+    rims_grad = Swap(me, send_e, in_e, swap_sems.at[3])
     reduce_one = Sum(place, rest[:9], one_sems)
     reduce_two = Sum(place, rest[9:18], two_sems)
 
-    make_plan(me, order_ref, slot_ref, near_ref, turn_ref, flag_ref, table)
+    tile_in, found, over_count = plan_sends(me, order_ref, slot_ref, near_ref, turn_ref, table)
     loads[0].wait()
     loads[1].wait()
     for slot in range(2):
@@ -892,6 +925,7 @@
     send_thin(table, thin_strips, thin_corners, send_a)
     pl.semaphore_wait(barrier, 29)
     rims_one.start()
+    plan_pieces(me, tile_in, found, slot_ref, near_ref, turn_ref, flag_ref, table)
 
     grad_wide[...] = jnp.zeros_like(grad_wide)
     loads[2].wait()
@@ -909,27 +943,40 @@
             grad_corners[at] = grad_corners[at] * keep
     send_rims(table, grad_strips, grad_corners, send_e, T_GIVE_STRIP, T_GIVE_CORNER)
     rims_grad.start()
+    plan_sums(found, over_count, table)
 
     loads[3].wait()
-    forward[...] = jnp.zeros_like(forward)
-    flipped[...] = jnp.zeros_like(flipped)
-    for layer in range(2):
+
+    def build_forward(layer):
+        forward[layer] = jnp.zeros(forward.shape[1:], BF16)
         for up in range(3):
             for across in range(3):
-                weight = kernels[layer, up, across]
-                turned = weight.T
                 for side in range(2):
                     at = (up * 4 + side + across) * 128
-                    forward[layer, at : at + 128, side * 128 : side * 128 + 128] = weight
+                    forward[layer, at : at + 128, side * 128 : side * 128 + 128] = kernels[layer, up, across]
+
+    def build_flipped(layer):
+        flipped[layer] = jnp.zeros(flipped.shape[1:], BF16)
+        for up in range(3):
+            for across in range(3):
+                turned = kernels[layer, up, across].T
+                for side in range(2):
                     at = (up * 4 + side + 2 - across) * 128
                     flipped[layer, at : at + 128, side * 128 : side * 128 + 128] = turned
-    for slot in range(2):
-        for row in (0, 5):
-            sources = [grad_wide[slot, row + 2 - up : row + 7 - up] for up in range(3)]
-            wide[slot, row : row + 5] = paired_conv(sources, 0, 5, flipped[1])
-        total[slot] = wide[slot, 1:9, 1:9]
-    give_back(table, wide, turns, send_b, given_strips, given_corners)
-    back_two.start()
+                if layer == 1:
+                    for edge in range(4):
+                        for step, tap in enumerate(STRIP_TAPS[edge]):
+                            if tap == (up, across):
+                                edge_weights[edge, step * 128 : step * 128 + 128] = turned
+                        if CORNER_TAPS[edge] == (up, across):
+                            corner_weights[:, edge * 128 : edge * 128 + 128] = turned
+
+    build_forward(0)
+    build_flipped(1)
+    for slot in range(2):
+        for row in (0, 4):
+            sources = [grad_wide[slot, row + 3 - up : row + 7 - up] for up in range(3)]
+            total[slot, row : row + 4] = paired_conv(sources, 1, 4, flipped[1])
 
     for slot in range(2):
         for step in range(4):
@@ -974,7 +1021,10 @@
     rims_two.start()
 
     rims_grad.wait()
-    extra = rim_terms(table, in_e, grad_strips, grad_corners, strips, corners, turns, masked)
+    extra = rim_terms(
+        table, in_e, grad_strips, grad_corners, strips, corners, turns,
+        edge_weights, corner_weights, masked, total,
+    )
     windows = []
     for slot in range(2):
         for row in (0, 4):
@@ -991,8 +1041,6 @@
         reduce_two.half_send[half, 36:37] = broken.astype(BF16)
     reduce_two.one()
 
-    back_two.wait()
-    take_back(table, in_b, given_strips, given_corners, total)
     for row in range(8):
         both = [total[slot, row].astype(BF16).astype(F32).reshape(16, 8, 128) for slot in range(2)]
         grad = (jnp.concatenate(both, axis=1) * slope[row]).astype(BF16)
@@ -1009,6 +1057,8 @@
     reduce_one.put(gradient_terms(turned_one, windows))
     reduce_one.one()
 
+    build_flipped(0)
+    build_forward(1)
     for row in range(9):
         low = grad_even[row, 2:18].astype(F32)
         high = grad_even[row + 1, 2:18].astype(F32)
@@ -1047,6 +1097,8 @@
     widen(table, hidden_blocks, strips, corners, in_c, turns, widened)
     finish(0)
     finish(1)
+    stores = [pltpu.make_async_copy(fresh, fresh_far, load_sems.at[5])]
+    stores[0].start()
     reduce_two.four()
     reduce_one.four()
     back_one.wait()
@@ -1055,10 +1107,14 @@
         present = jnp.where(table[T_PRESENT + slot] > 0, 1.0, 0.0)
         value = grad_blocks[slot].astype(F32) + total[slot]
         summed[slot] = (value * present).astype(BF16)
+    stores.append(pltpu.make_async_copy(summed, summed_far, load_sems.at[6]))
+    stores[1].start()
     reduce_two.five()
     reduce_one.five()
     reduce_two.end(sums, 1, over)
     reduce_one.end(sums, 0, None)
+    for store in stores:
+        store.wait()
 
 
 def settle(scale, fresh, summed, sums, back, next_state, cell_grad, kernel_grads):
@@ -1131,19 +1187,20 @@
             shape(TILES, BF16), shape(TILES, BF16), shape((2, UNITS, 16, 128), BF16), shape((1,), jnp.int32)
         ],
         in_specs=specs("ssssvaaaaavvv"),
-        out_specs=specs("vvvs"),
+        out_specs=specs("aavs"),
         scratch_shapes=[
+            vmem(TILES, BF16), vmem(TILES, BF16), vmem((4, 384, 128), BF16), vmem((128, 512), BF16),
             pltpu.SMEM((T_SIZE,), jnp.int32),
             vmem(NATURAL, BF16), vmem(NATURAL, BF16), vmem(kernels.shape, BF16), vmem(turns.shape, BF16),
-            vmem((16, 128, 128), BF16), pltpu.SemaphoreType.DMA((5,)), vmem((8, 4, 16, 128), BF16), vmem(CORNERS, F32),
+            vmem((16, 128, 128), BF16), pltpu.SemaphoreType.DMA((7,)), vmem((8, 4, 16, 128), BF16), vmem(CORNERS, F32),
             vmem(TILES, BF16), vmem(TILES, BF16), vmem(TILES, BF16),
             vmem(STRIPS, BF16), vmem(CORNERS, BF16), vmem(STRIPS, BF16), vmem(CORNERS, BF16),
             vmem(STRIPS, BF16), vmem(CORNERS, BF16),
         ]
         + [vmem(THIN_SENT, BF16)]
-        + [vmem(SENT, BF16)] * 4
+        + [vmem(SENT, BF16)] * 3
         + [vmem(THIN_SENT, BF16)]
-        + [vmem(SENT, BF16)] * 4
+        + [vmem(SENT, BF16)] * 3
         + [
             vmem((2, 1536, 256), BF16), vmem((2, 1536, 256), BF16),
             vmem((2, 12, 12, 16, 128), BF16), vmem((2, 10, 10, 16, 128), F32), vmem(TILES, F32),
@@ -1155,7 +1212,7 @@
         + sum_buffers()
         + sum_buffers()
         + [
-            pltpu.SemaphoreType.DMA((5, 2, 6)),
+            pltpu.SemaphoreType.DMA((4, 2, 6)),
             pltpu.SemaphoreType.DMA((2, 39)),
             pltpu.SemaphoreType.DMA((2, 39)),
         ],

time: 53.3 us -> 55 us (1.032)
  Pallas kernels: 49.3 us -> 50.9 us
    pallas_call x1, Pallas kernels: 47.5 us -> 49.1 us  [routed(): pl.pallas_call(whole, out_shape=[shape(TILES, BF16), shape(TILES, BF16),...]
where the time goes in v5:
time: 55 us; the launch traced here: 54.8 us
  Pallas kernels  50.9 us (93%)
  local copies, waits for them, and re-layouts  2.11 us (4%)
  between operations  1.46 us (3%)
    pallas_call x1, Pallas kernels, routed(): pl.pallas_call(whole, out_shape=[shape(TILES, BF16), shape(TILES, BF16),...  49.1 us
    pallas_call x1, Pallas kernels, finished(): pl.pallas_call(functools.partial(settle, scale), grid=(2,), out_shape=[sh...  1.83 us
    unnamed x20, local copies, waits for them, and re-layouts  1.36 us

profile of v5, /device:TPU:1, one launch (start us, length us, event | category | flops | bytes accessed | tf_op | source)
XLA Modules:
  0.0 54.8 jit_solution(18438897359855662316)
XLA Ops:
  0.6 0.0 copy-start.34
  0.6 0.0 copy-start.35
  0.7 0.0 copy-start.36
  0.7 0.0 copy-start.1
  0.7 0.0 copy-start.2
  0.7 0.0 copy-start.7
  0.7 0.0 copy-start.15
  0.7 49.1 %shard_map.155 = (bf16[2,8,8,16,128]{4,3,2,1,0:T(8,128)(2,1)}, bf16[2,8,8,16,128]{4,3,2,1,0:T(8,128)(2,1)}, bf16[2,72,16,128]{3,2,1,0:T(8,128)(2,1)}, s32[1]{0:T(128)}) custom-call(s32[192]{0:T(256)} %slot_ref.1, s32[8,192]{1,0:T(8,128)} %bitcast.685, s32[8,192]{1,0:T(8,128)} %bitcast.686, s32[4,192]{1,0:T(4,128)} %bitcast.687, s32[1,192]{1,0:T(1,128)} %bitcast.585, ...), custom_call_target="tpu_custom_call" | custom-call | tf_op jit(solution)/shard_map/pallas_call | solution.py:1184
  50.5 0.0 copy-done.34
  50.5 0.0 copy-done.35
  50.5 0.0 copy-done.36
  50.5 0.0 copy-done.1
  50.5 0.0 copy-done.2
  50.5 0.0 copy-done.7
  50.5 0.0 copy-done.15
  50.6 2.9 %conditional.1 = (f32[2,3,3,128,128]{4,3,2,1,0:T(8,128)S(1)}, bf16[1,2,32,32,128]{4,3,2,1,0:T(8,128)(2,1)S(1)}, bf16[1,2,32,32,128]{4,3,2,1,0:T(8,128)(2,1)S(1)}) conditional(s32[]{:T(128)} %bitcast.241, (s32[192]{0:T(256)S(1)}, bf16[1,2,32,32,128]{4,3,2,1,0:T(8,128)(2,1)S(1)}, s32[192,4]{0,1:T(4,128)S(1)}, s32[192,8]{0,1:T(8,128)S(1)}, ...), branch_computations={%region_0.10_spmd, %region_7.11_spmd} | conditional | flops 3985077248 | bytes 308919744 | solution.py:1234
  50.8 0.0 copy-start
  50.8 0.7 %copy-done = bf16[128,128]{1,0:T(8,128)(2,1)S(1)} copy-done((bf16[128,128]{1,0:T(8,128)(2,1)S(1)}, bf16[128,128]{1,0:T(8,128)(2,1)}, u32[]{:S(2)}) %copy-start) | copy-done | bytes 32792 | tf_op jit(solution)/shard_map/cond
  51.6 1.8 %branch_1_fun.1 = (bf16[16,128,128]{2,1,0:T(8,128)(2,1)S(1)}, bf16[16,128,128]{2,1,0:T(8,128)(2,1)S(1)}, f32[144,16,128]{2,1,0:T(8,128)S(1)}) custom-call(bf16[16,8,16,128]{3,2,1,0:T(8,128)(2,1)} %bitcast.649, bf16[16,8,16,128]{3,2,1,0:T(8,128)(2,1)} %bitcast.650, bf16[144,16,128]{2,1,0:T(8,128)(2,1)} %bitcast.648, bf16[128,128]{1,0:T(8,128)(2,1)S(1)} %copy-done), custom_call_target="tpu_custom_call" | custom-call | tf_op jit(solution)/shard_map/cond/branch_1_fun/pallas_call | solution.py:1160
  53.4 0.0 copy-start.12
  53.4 0.0 copy-start.19
  53.5 0.0 copy-start.20
  53.5 1.0 %copy-done.12 = f32[2,3,3,128,128]{4,3,2,1,0:T(8,128)} copy-done((f32[2,3,3,128,128]{4,3,2,1,0:T(8,128)}, f32[2,3,3,128,128]{4,3,2,1,0:T(8,128)S(1)}, u32[]{:S(2)}) %copy-start.12) | copy-done | bytes 1179672
  54.4 0.2 copy-done.19
  54.6 0.2 copy-done.20
Async XLA Ops:
  0.6 49.9 %copy-start.34 = (s32[192,8]{0,1:T(8,128)S(1)}, s32[192,8]{0,1:T(8,128)}, u32[]{:S(2)}) copy-start(s32[192,8]{0,1:T(8,128)} %param.25) | copy-start | bytes 18436
  0.6 49.9 %copy-start.35 = (s32[192,8]{0,1:T(8,128)S(1)}, s32[192,8]{0,1:T(8,128)}, u32[]{:S(2)}) copy-start(s32[192,8]{0,1:T(8,128)} %param.26) | copy-start | bytes 18436
  0.7 49.9 %copy-start.36 = (s32[192,4]{0,1:T(4,128)S(1)}, s32[192,4]{0,1:T(4,128)}, u32[]{:S(2)}) copy-start(s32[192,4]{0,1:T(4,128)} %param.27) | copy-start | bytes 9220
  0.7 49.9 %copy-start.1 = (s32[192]{0:T(256)S(1)}, s32[192]{0:T(256)}, u32[]{:S(2)}) copy-start(s32[192]{0:T(256)} %slot_ref.1) | copy-start | bytes 2308
  0.7 49.9 %copy-start.2 = (bf16[1,2,32,32,128]{4,3,2,1,0:T(8,128)(2,1)S(1)}, bf16[1,2,32,32,128]{4,3,2,1,0:T(8,128)(2,1)}, u32[]{:S(2)}) copy-start(bf16[1,2,32,32,128]{4,3,2,1,0:T(8,128)(2,1)} %param.21) | copy-start | bytes 1572868
  0.7 49.9 %copy-start.7 = (bf16[1,2,32,32,128]{4,3,2,1,0:T(8,128)(2,1)S(1)}, bf16[1,2,32,32,128]{4,3,2,1,0:T(8,128)(2,1)}, u32[]{:S(2)}) copy-start(bf16[1,2,32,32,128]{4,3,2,1,0:T(8,128)(2,1)} %param.22) | copy-start | bytes 1572868
  0.7 49.9 %copy-start.15 = (bf16[2,3,3,128,128]{4,3,2,1,0:T(8,128)(2,1)S(1)}, bf16[2,3,3,128,128]{4,3,2,1,0:T(8,128)(2,1)}, u32[]{:S(2)}) copy-start(bf16[2,3,3,128,128]{4,3,2,1,0:T(8,128)(2,1)} %kernels_far.1) | copy-start | bytes 1769476
  50.8 0.8 %copy-start = (bf16[128,128]{1,0:T(8,128)(2,1)S(1)}, bf16[128,128]{1,0:T(8,128)(2,1)}, u32[]{:S(2)}) copy-start(bf16[128,128]{1,0:T(8,128)(2,1)} %constant.181.clone.1.back) | copy-start | bytes 98308 | tf_op jit(solution)/shard_map/cond
  53.4 1.0 %copy-start.12 = (f32[2,3,3,128,128]{4,3,2,1,0:T(8,128)}, f32[2,3,3,128,128]{4,3,2,1,0:T(8,128)S(1)}, u32[]{:S(2)}) copy-start(f32[2,3,3,128,128]{4,3,2,1,0:T(8,128)S(1)} %get-tuple-element.186) | copy-start | bytes 3538948
  53.4 1.2 %copy-start.19 = (bf16[1,2,32,32,128]{4,3,2,1,0:T(8,128)(2,1)}, bf16[1,2,32,32,128]{4,3,2,1,0:T(8,128)(2,1)S(1)}, u32[]{:S(2)}) copy-start(bf16[1,2,32,32,128]{4,3,2,1,0:T(8,128)(2,1)S(1)} %get-tuple-element.188) | copy-start | bytes 1572868
  53.5 1.3 %copy-start.20 = (bf16[1,2,32,32,128]{4,3,2,1,0:T(8,128)(2,1)}, bf16[1,2,32,32,128]{4,3,2,1,0:T(8,128)(2,1)S(1)}, u32[]{:S(2)}) copy-start(bf16[1,2,32,32,128]{4,3,2,1,0:T(8,128)(2,1)S(1)} %get-tuple-element.187) | copy-start | bytes 1572868
